TPU v7x, 256 devices: a whole 4x4x8 slice. The times are simulated.
256 devices in a mesh: dp: 32 (over z, x), vocab: 8 (over y, core).
Axes of the slice: x: 4, y: 4, z: 8, core: 2. Of those that a mesh axis runs over, the one named last changes fastest.
Arguments:
- hidden: bfloat16 [256, 7168], P('dp'), may hold values from -12 to 12
- final_hidden: bfloat16 [256, 7168], P('dp'), may hold values from -12 to 12
- translator: bfloat16 [7168, 7168], P('dp', 'vocab'), may hold values from -0.0625 to 0.0625
- offset: float32 [7168], P('vocab'), may hold values from -3 to 3
- norm_gain: bfloat16 [7168], replicated, may hold values from 0.5 to 1.5
- unembed: bfloat16 [7168, 131072], P(None, ('dp', 'vocab')), may hold values from -1 to 1
Outputs:
- grad_translator: float32 [7168, 7168], P('dp', 'vocab')
- grad_offset: float32 [7168], P('vocab')
- divergence: float32 [256], P('dp')
All inputs are finite; a program needn't handle non-finite values.
Results may differ from a plain program's by a relative error of at most 0.0063.
Values may be sent and summed in bfloat16 or wider, within the bound.
A program may use at most 128 MiB of HBM per device.

v0:
```python
import jax
import jax.numpy as jnp
from jax import lax
from jax.sharding import PartitionSpec as P

D = 7168


EPSILON = 1e-06


def on_device(hidden, final_hidden, translator, offset, norm_gain, unembed):
    dev_row = lax.axis_index("dp")
    dev_col = lax.axis_index("vocab")
    col_width = translator.shape[1]
    own_tokens = hidden.shape[0]
    gain_all = norm_gain.astype(jnp.float32)
    gain_part = lax.dynamic_slice_in_dim(gain_all, dev_col * col_width, col_width, 0)
    cols_part = lax.dynamic_slice_in_dim(hidden, dev_col * col_width, col_width, 1)
    rows_all = lax.all_to_all(hidden, "dp", split_axis=1, concat_axis=0, tiled=True)
    cols_all = lax.all_gather(cols_part, "dp", axis=0, tiled=True)
    mapped = jnp.dot(rows_all, translator, preferred_element_type=jnp.float32)
    lens_state = cols_all.astype(jnp.float32) + lax.psum(mapped, "dp") + offset
    final_all = lax.all_gather(final_hidden, "dp", axis=0, tiled=True).astype(jnp.float32)
    lens_sq = lax.psum(jnp.sum(lens_state * lens_state, axis=1), "vocab")
    inverse_rms = lax.rsqrt(lens_sq / D + EPSILON)[:, None]
    lens_piece = (lens_state * inverse_rms * gain_part).astype(jnp.bfloat16)
    lens_in = lax.all_gather(lens_piece, "vocab", axis=1, tiled=True)
    final_inverse = lax.rsqrt(jnp.mean(final_all * final_all, axis=1, keepdims=True) + EPSILON)
    final_in = (final_all * final_inverse * gain_all).astype(jnp.bfloat16)
    lens_logits = jnp.dot(lens_in, unembed, preferred_element_type=jnp.float32)
    final_logits = jnp.dot(final_in, unembed, preferred_element_type=jnp.float32)
    lens_peak, final_peak = lax.pmax(
        (jnp.max(lens_logits, axis=1), jnp.max(final_logits, axis=1)), ("dp", "vocab")
    )
    final_weight = jnp.exp(final_logits - final_peak[:, None])
    lens_sum, final_sum, cross_term = lax.psum(
        (
            jnp.sum(jnp.exp(lens_logits - lens_peak[:, None]), axis=1),
            jnp.sum(final_weight, axis=1),
            jnp.sum(final_weight * (final_logits - lens_logits), axis=1),
        ),
        ("dp", "vocab"),
    )
    lens_total = lens_peak + jnp.log(lens_sum)
    final_total = final_peak + jnp.log(final_sum)
    divergence_all = cross_term / final_sum + lens_total - final_total
    logit_grad = (
        jnp.exp(lens_logits - lens_total[:, None]) - jnp.exp(final_logits - final_total[:, None])
    ).astype(jnp.bfloat16)
    partial_grad = lax.psum_scatter(
        lax.dot_general(
            unembed, logit_grad, (((1,), (1,)), ((), ())), preferred_element_type=jnp.float32
        ),
        "vocab",
        scatter_dimension=0,
        tiled=True,
    )
    state_grad = lax.psum(partial_grad, "dp").T
    weighted = gain_part * state_grad
    slope_term = lax.psum(jnp.sum(weighted * lens_state, axis=1), "vocab")[:, None] / D
    state_delta = inverse_rms * weighted - lens_state * inverse_rms**3 * slope_term
    grad_translator = lax.dot_general(
        rows_all,
        state_delta.astype(jnp.bfloat16),
        (((0,), (0,)), ((), ())),
        preferred_element_type=jnp.float32,
    )
    grad_offset = jnp.sum(state_delta, axis=0)
    divergence = lax.dynamic_slice_in_dim(divergence_all, dev_row * own_tokens, own_tokens, 0)
    return (grad_translator, grad_offset, divergence)


def solution(mesh):
    placed = (
        P("dp", None),
        P("dp", None),
        P("dp", "vocab"),
        P("vocab"),
        P(),
        P(None, ("dp", "vocab")),
    )
    return jax.shard_map(
        on_device,
        mesh=mesh,
        in_specs=placed,
        out_specs=(P("dp", "vocab"), P("vocab"), P("dp")),
        check_vma=False,
    )
```

profile of v0, /device:TPU:1, one launch (start us, length us, event | category | flops | bytes accessed | tf_op | source)
XLA Modules:
  0.0 677.1 jit_solution(13700832516033778749)
XLA Ops:
  7.2 1.1 all_to_all.14
  8.4 0.1 copy.9
  8.5 21.0 %all_to_all.19 = bf16[8,32,224]{2,0,1:T(8,128)(2,1)S(1)} all-to-all(bf16[8,32,224]{2,0,1:T(8,128)(2,1)S(1)} %copy.9), channel_id=1, replica_groups=mesh['dp'=32,'vocab'=8] {'dp'}, dimensions={1} | all-to-all | bytes 229376 | tf_op jit(solution)/shard_map/all_to_all | solution.py:20
  29.5 1.2 fusion.14
  30.7 0.0 all-gather.5.cloned.1.call-start
  30.8 0.7 all-gather.5.cloned.1.call-update
  31.5 0.0 all-gather.3.cloned.1.call-start
  31.5 0.8 dynamic_slice.10
  32.3 0.7 constant_dynamic-slice_fusion
  33.0 36.8 %all_gather.9 = bf16[256,896]{1,0:T(8,128)(2,1)S(1)} all-gather(bf16[8,896]{1,0:T(8,128)(2,1)S(1)} %constant_dynamic-slice_fusion), channel_id=1, replica_groups=mesh['dp'=32,'vocab'=8] {'dp'}, dimensions={0}, use_global_device_ids=true | all-gather | bytes 473088 | tf_op jit(solution)/shard_map/all_gather | solution.py:21
  69.8 102.5 %all-reduce.5.cloned.1.call-done = f32[256,896]{1,0:T(8,128)} async-done(((f32[256,896]{1,0:T(8,128)}), f32[256,896]{1,0:T(8,128)}) %all-reduce.5.cloned.1.call-update) | async-done | bytes 917520 | tf_op jit(solution)/shard_map/psum | solution.py:23
  172.4 1.4 multiply_reduce_fusion
  173.8 17.1 %psum.50 = f32[256]{0:T(256)S(1)} all-reduce(f32[256]{0:T(256)S(1)} %multiply_reduce_fusion), channel_id=1, replica_groups=mesh['dp'=32,'vocab'=8] {'vocab'}, use_global_device_ids=true, to_apply=%region_2.0 | all-reduce | flops 256 | bytes 2048 | tf_op jit(solution)/shard_map/psum | solution.py:25
  190.9 2.2 multiply_convert_fusion
  193.1 0.0 reduce-scatter.2.cloned.1.call-start
  193.1 60.9 %all-gather.5.cloned.1.call-done = bf16[256,7168]{1,0:T(8,128)(2,1)} async-done(((bf16[8,7168]{1,0:T(8,128)(2,1)}), bf16[256,7168]{1,0:T(8,128)(2,1)}) %all-gather.5.cloned.1.call-update) | async-done | bytes 3670032 | tf_op jit(solution)/shard_map/all_gather | solution.py:24
  254.0 2.8 fusion
  256.9 6.4 fusion.18
  263.3 26.2 %all-gather.3.cloned.1.call-done = bf16[256,7168]{1,0:T(8,128)(2,1)} async-done(((bf16[256,896]{1,0:T(8,128)(2,1)}), bf16[256,7168]{1,0:T(8,128)(2,1)}) %all-gather.3.cloned.1.call-update) | async-done | bytes 3670032 | tf_op jit(solution)/shard_map/all_gather | solution.py:28
  289.5 6.3 fusion.19
  295.8 76.1 %all-reduce.1 = (f32[256]{0:T(256)S(1)}, f32[256]{0:T(256)S(1)}) all-reduce(f32[256]{0:T(256)S(1)} %get-tuple-element.18, f32[256]{0:T(256)S(1)} %get-tuple-element.20), channel_id=1, replica_groups=mesh['dp'=32,'vocab'=8] {'dp','vocab'}, use_global_device_ids=true, to_apply=%region_9.0 | all-reduce | flops 512 | bytes 4096 | tf_op jit(solution)/shard_map/pmax | solution.py:33
  371.9 0.4 multiply_reduce_fusion.1
  372.3 74.2 %all-reduce = (f32[256]{0:T(256)S(1)}, f32[256]{0:T(256)S(1)}, f32[256]{0:T(256)S(1)}) all-reduce(f32[256]{0:T(256)S(1)} %get-tuple-element.4, f32[256]{0:T(256)S(1)} %get-tuple-element.5, f32[256]{0:T(256)S(1)} %get-tuple-element.3), channel_id=1, replica_groups=mesh['dp'=32,'vocab'=8] {'dp','vocab'}, use_global_device_ids=true, to_apply=%region_11.0 | all-reduce | flops 768 | bytes 6144 | tf_op jit(solution)/shard_map/psum | solution.py:37
  446.6 8.2 %convolution_bitcast_fusion = f32[7168,256]{0,1:T(8,128)} fusion(bf16[7168,512]{1,0:T(8,128)(2,1)} %param.11, f32[256,512]{1,0:T(8,128)S(1)} %get-tuple-element.19, f32[256,512]{1,0:T(8,128)S(1)} %get-tuple-element.21, f32[256]{0:T(256)S(1)} %get-tuple-element.15, f32[256]{0:T(256)S(1)} %get-tuple-element.12), kind=kOutput, calls=%fused_computation | convolution fusion | flops 1879572480 | bytes 15730688 | tf_op jit(solution)/shard_map/dot_general | solution.py:52
  454.8 0.0 all-reduce.7.cloned.1.call-start
  454.9 45.7 %reduce-scatter.2.cloned.1.call-done = f32[896,256]{0,1:T(8,128)} async-done(((f32[7168,256]{0,1:T(8,128)}), f32[896,256]{0,1:T(8,128)}) %reduce-scatter.2.cloned.1.call-update) | async-done | bytes 917520 | tf_op jit(solution)/shard_map/reduce_scatter | solution.py:51
  500.6 0.6 dynamic_slice.11
  501.2 147.5 %all-reduce.7.cloned.1.call-done = f32[896,256]{0,1:T(8,128)} async-done(((f32[896,256]{0,1:T(8,128)}), f32[896,256]{0,1:T(8,128)}) %all-reduce.7.cloned.1.call-update) | async-done | bytes 917520 | tf_op jit(solution)/shard_map/psum | solution.py:59
  648.7 1.5 fusion.8
  650.1 17.1 %psum.54 = f32[256]{0:T(256)S(1)} all-reduce(f32[256]{0:T(256)S(1)} %fusion.8), channel_id=1, replica_groups=mesh['dp'=32,'vocab'=8] {'vocab'}, use_global_device_ids=true, to_apply=%region_15.0 | all-reduce | flops 256 | bytes 2048 | tf_op jit(solution)/shard_map/psum | solution.py:61
  667.2 2.1 fusion.16
  669.3 1.2 convolution_bitcast_fusion.1
  (18 shorter events, 0.2 us)
Async XLA Ops:
  7.2 22.3 %copy-start = (bf16[224,896]{1,0:T(8,128)(2,1)S(1)}, bf16[224,896]{1,0:T(8,128)(2,1)}, u32[]{:S(2)}) copy-start(bf16[224,896]{1,0:T(8,128)(2,1)} %param.8) | copy-start | bytes 1204228
  7.2 185.9 %copy-start.3 = (bf16[7168]{0:T(1024)(128)(2,1)S(1)}, bf16[7168]{0:T(1024)(128)(2,1)}, u32[]{:S(2)}) copy-start(bf16[7168]{0:T(1024)(128)(2,1)} %param.10) | copy-start | bytes 43012
  7.2 165.2 %all-reduce.5.cloned.1.call-start = ((), (), s32[]{:S(2)}) async-start(), calls=%async_computation.2 | async-start | bytes 1835008 | tf_op jit(solution)/shard_map/psum | solution.py:23
  30.7 223.3 %all-gather.5.cloned.1.call-start = ((), (), s32[]{:S(2)}) async-start(), calls=%async_computation.4 | async-start | bytes 3784704 | tf_op jit(solution)/shard_map/all_gather | solution.py:24
  31.5 258.0 %all-gather.3.cloned.1.call-start = ((), (), s32[]{:S(2)}) async-start(), calls=%async_computation.3 | async-start | bytes 4128768 | tf_op jit(solution)/shard_map/all_gather | solution.py:28
  193.1 307.5 %reduce-scatter.2.cloned.1.call-start = ((), (), s32[]{:S(2)}) async-start(), calls=%async_computation.5 | async-start | bytes 8257536 | tf_op jit(solution)/shard_map/reduce_scatter | solution.py:51
  454.8 193.9 %copy-start.1 = (f32[256,896]{1,0:T(8,128)S(1)}, f32[256,896]{1,0:T(8,128)}, u32[]{:S(2)}) copy-start(f32[256,896]{1,0:T(8,128)} %all-reduce.5.cloned.1.call-done) | copy-start | bytes 2752516
  454.8 193.9 %copy-start.2 = (f32[896]{0:T(1024)S(1)}, f32[896]{0:T(1024)}, u32[]{:S(2)}) copy-start(f32[896]{0:T(1024)} %param.9) | copy-start | bytes 10756
  454.8 193.9 %all-reduce.7.cloned.1.call-start = ((), (), s32[]{:S(2)}) async-start(), calls=%async_computation.6 | async-start | bytes 1835008 | tf_op jit(solution)/shard_map/psum | solution.py:59
Sparse Core Ops, SparseCore 0:
  30.9 141.4 all-reduce.4
  174.9 79.0 all-gather.4
  256.4 33.0 all-gather.2
  454.9 45.6 reduce-scatter.1
  503.9 144.7 all-reduce.6
where the time goes:
time: 678 us; the launch traced here: 677 us
  waiting for transfers between devices  384 us (57%)
  blocking collectives  242 us (36%)
  matrix products  23.4 us (3%)
  between operations  13.9 us (2%)
  other arithmetic  10.5 us (2%)
    psum x1, waiting for transfers between devices, on_device(): state_grad = lax.psum(partial_grad, 'dp').T  147 us
    psum x1, waiting for transfers between devices, on_device(): lens_state = cols_all.astype(jnp.float32) + lax.psum(mapped, 'dp') + offset  103 us
    pmax x1, blocking collectives, on_device(): lax.pmax((jnp.max(lens_logits, axis=1), jnp.max(final_logits, axis=1)), (...  76.1 us
    psum x1, blocking collectives, on_device(): lax.psum((jnp.sum(jnp.exp(lens_logits - lens_peak[:, None]), axis=1), jnp...  74.2 us
    all_gather x1, waiting for transfers between devices, on_device(): lax.all_gather(final_hidden, 'dp', axis=0, tiled=True).astype(jnp.float32)  60.9 us
    reduce_scatter x1, waiting for transfers between devices, on_device(): lax.psum_scatter(lax.dot_general(unembed, logit_grad, (((1,), (1,)), ((),...  45.7 us
    all_gather x1, blocking collectives, on_device(): cols_all = lax.all_gather(cols_part, 'dp', axis=0, tiled=True)  36.8 us
    all_gather x1, waiting for transfers between devices, on_device(): lens_in = lax.all_gather(lens_piece, 'vocab', axis=1, tiled=True)  26.2 us
  transfers between devices with their start and end apart: 5, of which 5 were waited for; matrix products, arithmetic and copies ran while one was open for 2% of the time, Pallas kernels for 0%

commit v1 on v0

v1 whole, which is shorter than its diff:
```python
import functools

import jax
import jax.numpy as jnp
from jax import lax
from jax.experimental import pallas as pl
from jax.experimental.pallas import tpu as pltpu
from jax.sharding import PartitionSpec as P

MESH = pl.DeviceIdType.MESH
F32, BF16 = jnp.float32, jnp.bfloat16
D = 7168
COLS = 896
ROWS = 224
VOC = 512
EPSILON = 1e-06
NZ, NX, NY = 8, 4, 4


def pack(a):
    low = jnp.concatenate([a[:, 512:], jnp.zeros((8, 128), F32)], axis=1)
    return jnp.concatenate([a[:, :512], low], axis=0).astype(BF16)


def unpack(blocks):
    wide = blocks.astype(F32)
    return jnp.concatenate([wide[:, :8], wide[:, 8:, :384]], axis=2).reshape(64, COLS).astype(BF16)


def merge(tiles):
    lens_peak = functools.reduce(jnp.maximum, [t[0:1] for t in tiles])
    final_peak = functools.reduce(jnp.maximum, [t[2:3] for t in tiles])
    lens_sum = sum(t[1:2] * jnp.exp(t[0:1] - lens_peak) for t in tiles)
    scales = [jnp.exp(t[2:3] - final_peak) for t in tiles]
    final_sum = sum(t[3:4] * s for t, s in zip(tiles, scales))
    cross = sum(t[4:5] * s for t, s in zip(tiles, scales))
    return stack_rows([lens_peak, lens_sum, final_peak, final_sum, cross])


def stack_rows(rows):
    place = lax.broadcasted_iota(jnp.int32, (8, 256), 0)
    tile = jnp.zeros((8, 256), F32)
    for i, row in enumerate(rows):
        tile = jnp.where(place == i, jnp.broadcast_to(row, (8, 256)), tile)
    return tile


def kernel(
    hid, fin, tw, off, gain, unemb, gt, goff, div,
    u, hpack, ha, xsend, hx, rows_t, twp, mapped, cx, sx, dz,
    f_norm, f_pack, f_z, f_buf, l_pack, l_z, l_buf, l_state,
    v_send, v_recv, w_send, w_recv,
    l_log, f_log, st_core, st_y, st_x, st_z, cols, grad,
    c_send, c_recv, acc, ry0, rx1, r0, r1, rx0, ry1, sz, rz,
    sd_pack, sd_z, sd,
    u_sem, a_s, a_r, b_s, b_r, c_s, c_r, d_s, d_r, v_s, v_r, w_s, w_r,
    fz_s, fz_r, f1_s, f1_r, f2_s, f2_r, fc_s, fc_r,
    lz_s, lz_r, l1_s, l1_r, l2_s, l2_r, lc_s, lc_r,
    tc_s, tc_r, ty_s, ty_r, tx_s, tx_r, tz_s, tz_r,
    gc_s, gc_r, g1_s, g1_r, g2_s, g2_r, gz_s, gz_r,
    oz_s, oz_r, ox_s, ox_r,
):
    r, c = lax.axis_index("dp"), lax.axis_index("vocab")
    z, x = lax.div(r, NX), lax.rem(r, NX)
    y, k = lax.div(c, 2), lax.rem(c, 2)
    half, quarter = lax.div(z, 4), lax.rem(z, 4)
    feat = pl.ds(pl.multiple_of(c * COLS, 128), COLS)

    def at_z(i):
        return (i * NX + x, c)

    def at_x(i):
        return (z * NX + i, c)

    def at_y(i):
        return (r, i * 2 + k)

    sibling = (r, y * 2 + (1 - k))
    unsent = []

    def copy(src, dst, ss, rs, dev):
        return pltpu.make_async_remote_copy(
            src_ref=src, dst_ref=dst, send_sem=ss, recv_sem=rs, device_id=dev, device_id_type=MESH
        )

    def send(src, dst, ss, rs, dev):
        one = copy(src, dst, ss, rs, dev)
        one.start()
        unsent.append(one)

    def recv(land, ss, rs, dev):
        copy(land, land, ss, rs, dev).wait_recv()

    def others(n, me):
        return [(d - 1, lax.rem(me + d, n), lax.rem(me + (n - d), n)) for d in range(1, n)]

    barrier = pltpu.get_barrier_semaphore()
    partners = [at_z(t) for _, t, _ in others(NZ, z)] + [at_x(t) for _, t, _ in others(NX, x)]
    group = [(d - 1, (r, lax.rem(c + d, 8)), (r, lax.rem(c + (8 - d), 8))) for d in range(1, 8)]
    partners += [t for _, t, _ in group]
    for p in partners:
        pl.semaphore_signal(barrier, inc=1, device_id=p, device_id_type=MESH)
    load_u = pltpu.make_async_copy(unemb, u, u_sem)
    load_u.start()

    for i in range(NZ):
        hpack[i] = pack(hid[:, i * COLS : (i + 1) * COLS].astype(F32))
    wide = fin[...].astype(F32)
    final_inverse = lax.rsqrt(jnp.sum(wide * wide, axis=1, keepdims=True) / D + EPSILON)
    f_norm[...] = wide * final_inverse * gain[...].astype(F32)
    f_pack[...] = pack(f_norm[:, feat])
    twp[:ROWS] = tw[...]
    twp[ROWS:] = jnp.zeros((256 - ROWS, COLS), BF16)
    pl.semaphore_wait(barrier, len(partners))

    for j, t, _ in others(NZ, z):
        send(hpack.at[t], ha.at[z], a_s.at[j], a_r.at[j], at_z(t))
    for j, t, _ in others(NZ, z):
        send(f_pack, f_z.at[z], fz_s.at[j], fz_r.at[j], at_z(t))
    ha[z] = hpack[z]
    f_z[z] = f_pack[...]
    for j, _, s in others(NZ, z):
        recv(ha.at[s], a_s.at[j], a_r.at[j], at_z(s))
    flat = unpack(ha[...]).astype(F32)
    for i in range(NX):
        part = jnp.concatenate([flat[:, i * ROWS : (i + 1) * ROWS], jnp.zeros((64, 256 - ROWS), F32)], axis=1)
        xsend[i] = part.astype(BF16).reshape(2, 32, 256)
    for j, t, _ in others(NX, x):
        send(xsend.at[t], hx.at[:, x], b_s.at[j], b_r.at[j], at_x(t))
    hx[:, x] = xsend[x]


    def own_pieces(buf, zbuf, zs, zr, s1, r1, s2, r2, sc, rc, firsts):
        for j, _, s in others(NZ, z):
            recv(zbuf.at[s], zs.at[j], zr.at[j], at_z(s))
        flat = unpack(zbuf[...])
        for h in range(2):
            buf[k, y, h, x] = flat[h * 32 : (h + 1) * 32]
        for h, first in enumerate(firsts):
            piece = buf.at[k, y, h, x]
            ways = [(NX, x, at_x), (NY, y, at_y)]
            (n1, m1, at1), (n2, m2, at2) = ways if first == "x" else ways[::-1]
            for j, t, _ in others(n1, m1):
                send(piece, piece, s1.at[h, j], r1.at[h, j], at1(t))
            for j, t, _ in others(n2, m2):
                send(piece, piece, s2.at[h, 0, j], r2.at[h, 0, j], at2(t))
            send(piece, piece, sc.at[h, 0, 0], rc.at[h, 0, 0], sibling)

    def forward(buf, s1, r1, s2, r2, sc, rc, firsts):
        for q in range(1, 4):
            for h, first in enumerate(firsts):
                if first == "x":
                    s = lax.rem(x + (NX - q), NX)
                    piece, dev, n2, m2, at2 = buf.at[k, y, h, s], at_x(s), NY, y, at_y
                    slot = (h, 0, q)
                else:
                    s = lax.rem(y + (NY - q), NY)
                    piece, dev, n2, m2, at2 = buf.at[k, s, h, x], at_y(s), NX, x, at_x
                    slot = (h, q, 0)
                recv(piece, s1.at[h, q - 1], r1.at[h, q - 1], dev)
                for j, t, _ in others(n2, m2):
                    send(piece, piece, s2.at[h, q, j], r2.at[h, q, j], at2(t))
                send(piece, piece, sc.at[slot], rc.at[slot], sibling)

    def rest(buf, s2, r2, sc, rc, firsts, each=lambda q: None):
        for q in range(1, 4):
            for j in range(4):
                for h, first in enumerate(firsts):
                    if first == "x":
                        yy, xx = lax.rem(y + (NY - q), NY), lax.rem(x + (NX - j), NX)
                        dev, slot = at_y(yy), (h, q, j)
                    else:
                        yy, xx = lax.rem(y + (NY - j), NY), lax.rem(x + (NX - q), NX)
                        dev, slot = at_x(xx), (h, j, q)
                    piece = buf.at[k, yy, h, xx]
                    recv(piece, s2.at[h, j, q - 1], r2.at[h, j, q - 1], dev)
                    send(piece, piece, sc.at[slot], rc.at[slot], sibling)
            each(q)

    def logits(buf, log, kk, yy):
        block = pl.ds(pl.multiple_of((yy * 2 + kk) * COLS, 128), COLS)
        log[...] += jnp.dot(buf[kk, yy].reshape(256, COLS), u[block, :], preferred_element_type=F32)

    def own_logits(buf, log):
        def step(q, _):
            logits(buf, log, k, lax.rem(y + (NY - q), NY))
            return 0

        lax.fori_loop(0, NY, step, 0)

    def sibling_logits(buf, log, sc, rc):
        def step(q, _):
            yy = lax.rem(y + (NY - q), NY)
            for h in range(2):
                for j in range(4):
                    xx = lax.rem(x + (NX - j), NX)
                    recv(buf.at[1 - k, yy, h, xx], sc.at[h, q, j], rc.at[h, q, j], sibling)
            logits(buf, log, 1 - k, yy)
            return 0

        lax.fori_loop(0, NY, step, 0)

    f_first, l_first = ("x", "x"), ("x", "y")
    own_pieces(f_buf, f_z, fz_s, fz_r, f1_s, f1_r, f2_s, f2_r, fc_s, fc_r, f_first)

    for j, _, s in others(NX, x):
        recv(hx.at[:, s], b_s.at[j], b_r.at[j], at_x(s))
    rows = hx[...].reshape(256, 256)
    mapped[...] = jnp.dot(rows, twp[...], preferred_element_type=F32).reshape(2, NX, 32, COLS)
    for j, t, _ in others(NX, x):
        send(mapped.at[:, t], cx.at[j], c_s.at[j], c_r.at[j], at_x(t))
    rows_t[...] = rows.astype(F32).T.astype(BF16)
    forward(f_buf, f1_s, f1_r, f2_s, f2_r, fc_s, fc_r, f_first)
    l_log[...] = jnp.zeros_like(l_log)
    f_log[...] = jnp.zeros_like(f_log)
    for j, t, s in others(NX, x):
        recv(cx.at[j], c_s.at[j], c_r.at[j], at_x(s))
    sx[...] = (mapped[:, x] + cx[0] + cx[1] + cx[2]).reshape(NZ, 8, COLS)
    for j, t, _ in others(NZ, z):
        send(sx.at[t], dz.at[j], d_s.at[j], d_r.at[j], at_z(t))
    base = hid[:, feat].astype(F32) + off[...] + sx[z]
    gain_part = gain[:, feat].astype(F32)
    for j, _, s in others(NZ, z):
        recv(dz.at[j], d_s.at[j], d_r.at[j], at_z(s))
        base = base + dz[j]
    l_state[...] = base

    def group_sum(part, snd, rcv, ss, rs):
        snd[...] = jnp.broadcast_to(part, (8, 128))
        for j, t, _ in group:
            send(snd, rcv.at[j], ss.at[j], rs.at[j], t)
        total = snd[...]
        for j, _, s in group:
            recv(rcv.at[j], ss.at[j], rs.at[j], s)
            total = total + rcv[j]
        return total[:, 0:1]

    squares = group_sum(jnp.sum(base * base, axis=1, keepdims=True), v_send, v_recv, v_s, v_r)
    inverse = lax.rsqrt(squares / D + EPSILON)
    l_pack[...] = pack(l_state[...] * inverse * gain_part)
    for j, t, _ in others(NZ, z):
        send(l_pack, l_z.at[z], lz_s.at[j], lz_r.at[j], at_z(t))
    l_z[z] = l_pack[...]
    load_u.wait()
    rest(f_buf, f2_s, f2_r, fc_s, fc_r, f_first)
    own_pieces(l_buf, l_z, lz_s, lz_r, l1_s, l1_r, l2_s, l2_r, lc_s, lc_r, l_first)
    own_logits(f_buf, f_log)
    forward(l_buf, l1_s, l1_r, l2_s, l2_r, lc_s, lc_r, l_first)
    sibling_logits(f_buf, f_log, fc_s, fc_r)
    rest(l_buf, l2_s, l2_r, lc_s, lc_r, l_first)
    own_logits(l_buf, l_log)
    sibling_logits(l_buf, l_log, lc_s, lc_r)

    place = lax.broadcasted_iota(jnp.int32, (32, 128), 1)

    def local(i, _):
        part = pl.ds(pl.multiple_of(i * 32, 32), 32)
        a, b = l_log[part, :], f_log[part, :]
        a_peak, b_peak = jnp.max(a, axis=1, keepdims=True), jnp.max(b, axis=1, keepdims=True)
        weight = jnp.exp(b - b_peak)
        found = [
            a_peak, jnp.sum(jnp.exp(a - a_peak), axis=1, keepdims=True), b_peak,
            jnp.sum(weight, axis=1, keepdims=True), jnp.sum(weight * (b - a), axis=1, keepdims=True),
        ]
        tile = jnp.zeros((32, 128), F32)
        for n, v in enumerate(found):
            tile = jnp.where(place == n, jnp.broadcast_to(v, (32, 128)), tile)
        cols[part, :] = tile
        return 0

    lax.fori_loop(0, 8, local, 0)
    st_core[0] = cols[...].T[:8]
    send(st_core.at[0], st_core.at[1], tc_s, tc_r, sibling)
    recv(st_core.at[1], tc_s, tc_r, sibling)
    st_y[3] = merge([st_core[0], st_core[1]])
    for buf, n, me, at, ss, rs, nxt in (
        (st_y, NY, y, at_y, ty_s, ty_r, st_x),
        (st_x, NX, x, at_x, tx_s, tx_r, st_z),
        (st_z, NZ, z, at_z, tz_s, tz_r, None),
    ):
        for j, t, _ in others(n, me):
            send(buf.at[n - 1], buf.at[j], ss.at[j], rs.at[j], at(t))
        for j, _, s in others(n, me):
            recv(buf.at[j], ss.at[j], rs.at[j], at(s))
        found = merge([buf[j] for j in range(n)])
        if nxt is not None:
            nxt[nxt.shape[0] - 1] = found
    lens_total = found[0:1] + jnp.log(found[1:2])
    final_total = found[2:3] + jnp.log(found[3:4])
    apart = found[4:5] / found[3:4] + lens_total - final_total
    tall = jnp.concatenate([stack_rows([lens_total, final_total, apart]), jnp.zeros((120, 256), F32)], axis=0)
    cols[...] = tall.T
    mine = pl.ds(pl.multiple_of(half * 128 + x * 32 + quarter * 8, 8), 8)
    div[...] = jnp.broadcast_to(cols[mine, 2:3], (8, 128))

    def slopes(i, _):
        part = pl.ds(pl.multiple_of(i * 32, 32), 32)
        totals = cols[part, :]
        grad[part, :] = (
            jnp.exp(l_log[part, :] - totals[:, 0:1]) - jnp.exp(f_log[part, :] - totals[:, 1:2])
        ).astype(BF16)
        return 0

    lax.fori_loop(0, 8, slopes, 0)

    def back(yy, kk):
        block = pl.ds(pl.multiple_of((yy * 2 + kk) * COLS, 128), COLS)
        return lax.dot_general(
            grad[...], u[block, :], (((1,), (1,)), ((), ())), preferred_element_type=F32
        ).reshape(2, NX, 32, COLS)

    def away(i, _):
        c_send[i] = back(i, 1 - k)
        copy(c_send.at[i], c_recv.at[i], gc_s.at[i], gc_r.at[i], sibling).start()
        return 0

    lax.fori_loop(0, NY, away, 0)

    def home(i, _):
        acc[i] = back(i, k)
        copy(c_recv.at[i], c_recv.at[i], gc_s.at[i], gc_r.at[i], sibling).wait_recv()
        acc[i] += c_recv[i]
        return 0

    lax.fori_loop(0, NY, home, 0)
    for j, t, _ in others(NY, y):
        send(acc.at[t, 0], ry0.at[j], g1_s.at[0, j], g1_r.at[0, j], at_y(t))
    for j, t, _ in others(NX, x):
        send(acc.at[:, 1, t], rx1.at[j], g1_s.at[1, j], g1_r.at[1, j], at_x(t))
    for j, _, s in others(NY, y):
        recv(ry0.at[j], g1_s.at[0, j], g1_r.at[0, j], at_y(s))

    def add0(i, _):
        r0[i] = acc[y, 0, i] + ry0[0, i] + ry0[1, i] + ry0[2, i]
        return 0

    lax.fori_loop(0, NX, add0, 0)
    for j, t, _ in others(NX, x):
        send(r0.at[t], rx0.at[j], g2_s.at[0, j], g2_r.at[0, j], at_x(t))
    for j, _, s in others(NX, x):
        recv(rx1.at[j], g1_s.at[1, j], g1_r.at[1, j], at_x(s))

    def add1(i, _):
        r1[i] = acc[i, 1, x] + rx1[0, i] + rx1[1, i] + rx1[2, i]
        return 0

    lax.fori_loop(0, NY, add1, 0)
    for j, t, _ in others(NY, y):
        send(r1.at[t], ry1.at[j], g2_s.at[1, j], g2_r.at[1, j], at_y(t))
    for j, _, s in others(NX, x):
        recv(rx0.at[j], g2_s.at[0, j], g2_r.at[0, j], at_x(s))
    for j, _, s in others(NY, y):
        recv(ry1.at[j], g2_s.at[1, j], g2_r.at[1, j], at_y(s))
    sz[0:4] = (r0[x] + rx0[0] + rx0[1] + rx0[2]).reshape(4, 8, COLS)
    sz[4:8] = (r1[y] + ry1[0] + ry1[1] + ry1[2]).reshape(4, 8, COLS)
    for j, t, _ in others(NZ, z):
        send(sz.at[t], rz.at[j], gz_s.at[j], gz_r.at[j], at_z(t))
    state_grad = sz[z]
    for j, _, s in others(NZ, z):
        recv(rz.at[j], gz_s.at[j], gz_r.at[j], at_z(s))
        state_grad = state_grad + rz[j]

    weighted = gain_part * state_grad
    state = l_state[...]
    slope = group_sum(jnp.sum(weighted * state, axis=1, keepdims=True), w_send, w_recv, w_s, w_r) / D
    delta = inverse * weighted - state * (inverse * inverse * inverse * slope)
    sd_pack[...] = pack(delta)
    for j, t, _ in others(NZ, z):
        send(sd_pack, sd_z.at[z], oz_s.at[j], oz_r.at[j], at_z(t))
    sd_z[z] = sd_pack[...]
    for j, _, s in others(NZ, z):
        recv(sd_z.at[s], oz_s.at[j], oz_r.at[j], at_z(s))
    sd[:, x] = unpack(sd_z[...]).reshape(2, 32, COLS)
    for j, t, _ in others(NX, x):
        send(sd.at[:, x], sd.at[:, x], ox_s.at[j], ox_r.at[j], at_x(t))
    for j, _, s in others(NX, x):
        recv(sd.at[:, s], ox_s.at[j], ox_r.at[j], at_x(s))
    delta_all = sd[...].reshape(256, COLS)
    gt[...] = jnp.dot(rows_t[...], delta_all, preferred_element_type=F32)[:ROWS]
    goff[...] = jnp.sum(delta_all.astype(F32), axis=0, keepdims=True)

    for i in range(NY):
        copy(c_send.at[i], c_recv.at[i], gc_s.at[i], gc_r.at[i], sibling).wait_send()
    for one in unsent:
        one.wait_send()


def on_device(hidden, final_hidden, translator, offset, norm_gain, unembed):
    vm = pltpu.VMEM
    dma = pltpu.SemaphoreType.DMA
    blocks = [
        vm((D, VOC), BF16), vm((NZ, 16, 512), BF16), vm((NZ, 16, 512), BF16), vm((NX, 2, 32, 256), BF16),
        vm((2, NX, 32, 256), BF16), vm((256, 256), BF16), vm((256, COLS), BF16), vm((2, NX, 32, COLS), F32),
        vm((3, 2, 32, COLS), F32), vm((NZ, 8, COLS), F32), vm((7, 8, COLS), F32),
        vm((8, D), F32), vm((16, 512), BF16), vm((NZ, 16, 512), BF16), vm((2, NY, 2, NX, 32, COLS), BF16),
        vm((16, 512), BF16), vm((NZ, 16, 512), BF16), vm((2, NY, 2, NX, 32, COLS), BF16), vm((8, COLS), F32),
        vm((8, 128), F32), vm((7, 8, 128), F32), vm((8, 128), F32), vm((7, 8, 128), F32),
        vm((256, VOC), F32), vm((256, VOC), F32),
        vm((2, 8, 256), F32), vm((NY, 8, 256), F32), vm((NX, 8, 256), F32), vm((NZ, 8, 256), F32),
        vm((256, 128), F32), vm((256, VOC), BF16),
        vm((NY, 2, NX, 32, COLS), F32), vm((NY, 2, NX, 32, COLS), F32), vm((NY, 2, NX, 32, COLS), F32),
        vm((3, NX, 32, COLS), F32), vm((3, NY, 32, COLS), F32), vm((NX, 32, COLS), F32), vm((NY, 32, COLS), F32),
        vm((3, 32, COLS), F32), vm((3, 32, COLS), F32), vm((NZ, 8, COLS), F32), vm((7, 8, COLS), F32),
        vm((16, 512), BF16), vm((NZ, 16, 512), BF16), vm((2, NX, 32, COLS), BF16),
    ]
    pairs = [
        (7,), (3,), (3,), (7,), (7,), (7,),
        (7,), (2, 3), (2, 4, 3), (2, 4, 4),
        (7,), (2, 3), (2, 4, 3), (2, 4, 4),
        (), (3,), (3,), (7,),
        (4,), (2, 3), (2, 3), (7,),
        (7,), (3,),
    ]
    sems = [dma]
    for shape in pairs:
        sems += [dma(shape) if shape else dma] * 2
    whole = pl.BlockSpec(memory_space=pltpu.VMEM)
    gt, goff, div = pl.pallas_call(
        kernel,
        out_shape=(
            jax.ShapeDtypeStruct((ROWS, COLS), F32),
            jax.ShapeDtypeStruct((1, COLS), F32),
            jax.ShapeDtypeStruct((8, 128), F32),
        ),
        in_specs=[whole] * 5 + [pl.BlockSpec(memory_space=pl.ANY)],
        out_specs=(whole, whole, whole),
        scratch_shapes=blocks + sems,
        compiler_params=pltpu.CompilerParams(
            collective_id=0, has_side_effects=True, vmem_limit_bytes=56 * 2**20
        ),
        name="lens_step",
    )(hidden, final_hidden, translator, offset.reshape(1, COLS), norm_gain.reshape(1, D), unembed)
    return gt, goff.reshape(COLS), div[:, 0]


def solution(mesh):
    placed = (P("dp", None), P("dp", None), P("dp", "vocab"), P("vocab"), P(), P(None, ("dp", "vocab")))
    return jax.shard_map(
        on_device,
        mesh=mesh,
        in_specs=placed,
        out_specs=(P("dp", "vocab"), P("vocab"), P("dp")),
        check_vma=False,
    )
```

time: 678 us -> 159 us (0.23)
  waiting for transfers between devices: 384 us -> 0 us
  blocking collectives: 242 us -> 0 us
  Pallas kernels: 0 us -> 150 us
  matrix products: 23.4 us -> 0 us
  between operations: 13.9 us -> 0.64 us
  other arithmetic: 10.5 us -> 1.27 us
    psum x2 -> x0, waiting for transfers between devices: 250 us -> none  [the longest x1 147 us: on_device(): state_grad = lax.psum(partial_grad, 'dp').T]
    pallas_call x0 -> x1, Pallas kernels: none -> 150 us  [on_device(): pl.pallas_call(kernel, out_shape=(jax.ShapeDtypeStruct((ROWS, COLS), F32)...]
    psum x3 -> x0, blocking collectives: 108 us -> none  [the longest x1 74.2 us: on_device(): lax.psum((jnp.sum(jnp.exp(lens_logits - lens_peak[:, None]), axis=1), jnp...]
    all_gather x2 -> x0, waiting for transfers between devices: 87.1 us -> none  [the longest x1 60.9 us: on_device(): lax.all_gather(final_hidden, 'dp', axis=0, tiled=True).astype(jnp.float32)]
    pmax x1 -> x0, blocking collectives: 76.1 us -> none  [on_device(): lax.pmax((jnp.max(lens_logits, axis=1), jnp.max(final_logits, axis=1)), (...]
    reduce_scatter x1 -> x0, waiting for transfers between devices: 45.7 us -> none  [on_device(): lax.psum_scatter(lax.dot_general(unembed, logit_grad, (((1,), (1,)), ((),...]
    all_gather x1 -> x0, blocking collectives: 36.8 us -> none  [on_device(): cols_all = lax.all_gather(cols_part, 'dp', axis=0, tiled=True)]
    dot_general x5 -> x0, matrix products: 23.4 us -> none  [the longest x1 8.22 us: on_device(): lax.dot_general(unembed, logit_grad, (((1,), (1,)), ((), ())), preferred_...]
  transfers between devices with their start and end apart: 5 -> 0, of which waited for: 5 -> 0; matrix products, arithmetic and copies ran while one was open for 2% -> 0% of each run, Pallas kernels for 0% -> 0%
where the time goes in v1:
time: 159 us; the launch traced here: 158 us
  Pallas kernels  150 us (94%)
  local copies, waits for them, and re-layouts  5.98 us (4%)
    pallas_call x1, Pallas kernels, on_device(): pl.pallas_call(kernel, out_shape=(jax.ShapeDtypeStruct((ROWS, COLS), F32)...  150 us

profile of v1, /device:TPU:1, one launch (start us, length us, event | category | flops | bytes accessed | tf_op | source)
XLA Modules:
  0.0 158.1 jit_solution(7160297258449289633)
XLA Ops:
  0.6 1.3 reshape.15.off
  1.9 1.3 reshape.16.gain
  3.2 150.3 %lens_step.1 = (f32[224,896]{1,0:T(8,128)}, f32[1,896]{1,0:T(1,128)}, f32[8,128]{1,0:T(8,128)}) custom-call(bf16[8,7168]{1,0:T(8,128)(2,1)} %hid.1, bf16[8,7168]{1,0:T(8,128)(2,1)} %fin.1, bf16[224,896]{1,0:T(8,128)(2,1)} %tw.1, f32[1,896]{1,0:T(1,128)} %reshape.15.off, bf16[1,7168]{1,0:T(2,128)(2,1)} %reshape.16.gain, bf16[7168,512]{1,0:T(8,128)(2,1)} %unemb.1), custom_call_target="tpu_custom_call" | custom-call | tf_op jit(solution)/shard_map/lens_step/pallas_call | solution.py:418
  153.5 1.3 slice_reduce_fusion
  154.8 1.3 reduce
  156.1 2.1 %copy.10 = f32[224,896]{1,0:T(8,128)} copy(f32[224,896]{1,0:T(8,128)} %get-tuple-element.12) | data formatting | bytes 1605632

commit v2 on v1

v2 whole, which is shorter than its diff:
```python
import functools

import jax
import jax.numpy as jnp
from jax import lax
from jax.experimental import pallas as pl
from jax.experimental.pallas import tpu as pltpu
from jax.sharding import PartitionSpec as P

MESH = pl.DeviceIdType.MESH
F32, BF16 = jnp.float32, jnp.bfloat16
D = 7168
COLS = 896
ROWS = 224
VOC = 512
EPSILON = 1e-06
NZ, NX, NY = 8, 4, 4


def pack(a):
    low = jnp.concatenate([a[:, 512:], jnp.zeros((8, 128), F32)], axis=1)
    return jnp.concatenate([a[:, :512], low], axis=0).astype(BF16)


def unpack(blocks):
    wide = blocks.astype(F32)
    return jnp.concatenate([wide[:, :8], wide[:, 8:, :384]], axis=2).reshape(64, COLS).astype(BF16)


def merge(tiles):
    lens_peak = functools.reduce(jnp.maximum, [t[0:1] for t in tiles])
    final_peak = functools.reduce(jnp.maximum, [t[2:3] for t in tiles])
    lens_sum = sum(t[1:2] * jnp.exp(t[0:1] - lens_peak) for t in tiles)
    scales = [jnp.exp(t[2:3] - final_peak) for t in tiles]
    final_sum = sum(t[3:4] * s for t, s in zip(tiles, scales))
    cross = sum(t[4:5] * s for t, s in zip(tiles, scales))
    return stack_rows([lens_peak, lens_sum, final_peak, final_sum, cross])


def stack_rows(rows):
    place = lax.broadcasted_iota(jnp.int32, (8, 256), 0)
    tile = jnp.zeros((8, 256), F32)
    for i, row in enumerate(rows):
        tile = jnp.where(place == i, jnp.broadcast_to(row, (8, 256)), tile)
    return tile


def kernel(
    hid, fin, tw, off, gain, unemb, rows_out, sd_out, div,
    u, hpack, hin, twp, mapped, mapped_b, cx, sx, dz,
    f_norm, f_pack, f_z, f_buf, l_pack, l_z, l_buf, l_state, regain, squares,
    l_log, f_log, st_core, st_x, st_z, sl_core, sl_y, sl_x, sl_z, cols, inv_cols, sl_cols, grad,
    c_send, c_recv, acc, ry0, rx1, r0, r1, rx0, ry1, sz, rz,
    sd_z,
    u_sem, a_s, a_r, c_s, c_r, d_s, d_r,
    fz_s, fz_r, f1_s, f1_r, f2_s, f2_r, fc_s, fc_r,
    lz_s, lz_r, l1_s, l1_r, l2_s, l2_r, lc_s, lc_r,
    tc_s, tc_r, tx_s, tx_r, tz_s, tz_r,
    pc_s, pc_r, py_s, py_r, px_s, px_r, pz_s, pz_r,
    gc_s, gc_r, gy_s, gy_r, gx_s, gx_r, g2_s, g2_r, gz_s, gz_r,
    oz_s, oz_r, ox_s, ox_r,
):
    r, c = lax.axis_index("dp"), lax.axis_index("vocab")
    z, x = lax.div(r, NX), lax.rem(r, NX)
    y, k = lax.div(c, 2), lax.rem(c, 2)
    half, quarter = lax.div(z, 4), lax.rem(z, 4)
    feat = pl.ds(pl.multiple_of(c * COLS, 128), COLS)

    def at_z(i):
        return (i * NX + x, c)

    def at_x(i):
        return (z * NX + i, c)

    def at_y(i):
        return (r, i * 2 + k)

    sibling = (r, y * 2 + (1 - k))
    unsent = []

    def copy(src, dst, ss, rs, dev):
        return pltpu.make_async_remote_copy(
            src_ref=src, dst_ref=dst, send_sem=ss, recv_sem=rs, device_id=dev, device_id_type=MESH
        )

    def pair(sem):
        ss, rs, at = sem
        return (ss.at[at], rs.at[at]) if at else (ss, rs)

    def send(src, dst, sem, dev):
        one = copy(src, dst, *pair(sem), dev)
        one.start()
        unsent.append(one)

    def recv(land, sem, dev):
        copy(land, land, *pair(sem), dev).wait_recv()

    def others(n, me):
        return [(d - 1, lax.rem(me + d, n), lax.rem(me + (n - d), n)) for d in range(1, n)]

    barrier = pltpu.get_barrier_semaphore()
    def slot_of(i, j):
        return lax.div(i, 4) * 16 + j * 4 + lax.rem(i, 4)

    plane = []
    for i in range(NZ):
        for j in range(NX):
            if i + j:
                ahead = (lax.rem(z + i, NZ), lax.rem(x + j, NX))
                behind = (lax.rem(z + (NZ - i), NZ), lax.rem(x + (NX - j), NX))
                plane.append((len(plane), ahead, behind))
    partners = [(zz * NX + xx, c) for _, (zz, xx), _ in plane]
    group = [(d - 1, (r, lax.rem(c + d, 8)), (r, lax.rem(c + (8 - d), 8))) for d in range(1, 8)]
    partners += [t for _, t, _ in group]
    for p in partners:
        pl.semaphore_signal(barrier, inc=1, device_id=p, device_id_type=MESH)
    load_u = pltpu.make_async_copy(unemb, u, u_sem)
    load_u.start()

    flat = hid[...].astype(F32)
    for i in range(NZ * NX):
        low = jnp.concatenate([flat[:, i * ROWS + 128 : (i + 1) * ROWS], jnp.zeros((8, 32), F32)], axis=1)
        hpack[i] = jnp.concatenate([flat[:, i * ROWS : i * ROWS + 128], low], axis=0).astype(BF16)
    wide = fin[...].astype(F32)
    final_inverse = lax.rsqrt(jnp.sum(wide * wide, axis=1, keepdims=True) / D + EPSILON)
    gain_all = gain[...].astype(F32).reshape(1, D)
    f_norm[...] = wide * final_inverse * gain_all
    f_pack[...] = pack(f_norm[:, feat])
    for i in range(8):
        regain[i] = jnp.broadcast_to(1.0 / gain_all[:, i * COLS : (i + 1) * COLS], (8, COLS))
    twp[:ROWS] = tw[...]
    twp[ROWS:] = jnp.zeros((256 - ROWS, COLS), BF16)
    pl.semaphore_wait(barrier, len(partners))

    mine8 = slot_of(z, x)
    for j, (zz, xx), _ in plane:
        send(hpack.at[zz * NX + xx], hin.at[mine8], (a_s, a_r, (j,)), (zz * NX + xx, c))
    for j, t, _ in others(NZ, z):
        send(f_pack, f_z.at[z], (fz_s, fz_r, (j,)), at_z(t))
    hin[mine8] = hpack[r]
    f_z[z] = f_pack[...]

    f_first, l_first = ("x", "x"), ("x", "y")

    def own_pieces(buf, zbuf, zs, zr, s1, r1, s2, r2, sc, rc, firsts):
        for j, _, s in others(NZ, z):
            recv(zbuf.at[s], (zs, zr, (j,)), at_z(s))
        flat = unpack(zbuf[...])
        for h in range(2):
            buf[k, y, h, x] = flat[h * 32 : (h + 1) * 32]
        for h, first in enumerate(firsts):
            piece = buf.at[k, y, h, x]
            ways = [(NX, x, at_x), (NY, y, at_y)]
            (n1, m1, at1), (n2, m2, at2) = ways if first == "x" else ways[::-1]
            for j, t, _ in others(n1, m1):
                send(piece, piece, (s1, r1, (h, j)), at1(t))
            for j, t, _ in others(n2, m2):
                send(piece, piece, (s2, r2, (h, 0, j)), at2(t))
            send(piece, piece, (sc, rc, (h, 0, 0)), sibling)

    def forward(buf, s1, r1, s2, r2, sc, rc, firsts):
        for q in range(1, 4):
            for h, first in enumerate(firsts):
                if first == "x":
                    s = lax.rem(x + (NX - q), NX)
                    piece, dev, n2, m2, at2 = buf.at[k, y, h, s], at_x(s), NY, y, at_y
                    slot = (h, 0, q)
                else:
                    s = lax.rem(y + (NY - q), NY)
                    piece, dev, n2, m2, at2 = buf.at[k, s, h, x], at_y(s), NX, x, at_x
                    slot = (h, q, 0)
                recv(piece, (s1, r1, (h, q - 1)), dev)
                for j, t, _ in others(n2, m2):
                    send(piece, piece, (s2, r2, (h, q, j)), at2(t))
                send(piece, piece, (sc, rc, slot), sibling)

    def rest(buf, s2, r2, sc, rc, firsts, each=lambda q: None):
        for q in range(1, 4):
            for j in range(4):
                for h, first in enumerate(firsts):
                    if first == "x":
                        yy, xx = lax.rem(y + (NY - q), NY), lax.rem(x + (NX - j), NX)
                        dev, slot = at_y(yy), (h, q, j)
                    else:
                        yy, xx = lax.rem(y + (NY - j), NY), lax.rem(x + (NX - q), NX)
                        dev, slot = at_x(xx), (h, j, q)
                    piece = buf.at[k, yy, h, xx]
                    recv(piece, (s2, r2, (h, j, q - 1)), dev)
                    send(piece, piece, (sc, rc, slot), sibling)
            each(q)

    def logits(buf, log, kk, yy):
        cc = yy * 2 + kk
        block = pl.ds(pl.multiple_of(cc * COLS, 128), COLS)
        value = buf[kk, yy].reshape(256, COLS)
        log[...] += jnp.dot(value, u[block, :], preferred_element_type=F32)
        if buf is l_buf:
            scale = regain[cc][0:1]
            total = squares[...]
            for i in range(COLS // 128):
                lanes = slice(i * 128, (i + 1) * 128)
                plain = value[:, lanes].astype(F32) * scale[:, lanes]
                total = total + plain * plain
            squares[...] = total

    def own_logits(buf, log):
        def step(q, _):
            logits(buf, log, k, lax.rem(y + (NY - q), NY))
            return 0

        lax.fori_loop(0, NY, step, 0)

    def sibling_logits(buf, log, sc, rc):
        def step(q, _):
            yy = lax.rem(y + (NY - q), NY)
            for h in range(2):
                for j in range(4):
                    xx = lax.rem(x + (NX - j), NX)
                    recv(buf.at[1 - k, yy, h, xx], (sc, rc, (h, q, j)), sibling)
            logits(buf, log, 1 - k, yy)
            return 0

        lax.fori_loop(0, NY, step, 0)

    for j, _, (zz, xx) in plane:
        recv(hin.at[slot_of(zz, xx)], (a_s, a_r, (j,)), (zz * NX + xx, c))
    found = hin[...].astype(F32)
    rows = jnp.concatenate([found[:, :8].reshape(256, 128), found[:, 8:].reshape(256, 128)], axis=1)
    product = jnp.dot(rows.astype(BF16), twp[...], preferred_element_type=F32)
    mapped[...] = product.reshape(2, NX, 32, COLS)
    mapped_b[...] = product.astype(BF16).reshape(2, NX, 32, COLS)
    for j, t, _ in others(NX, x):
        send(mapped_b.at[:, t], cx.at[j], (c_s, c_r, (j,)), at_x(t))
    own_pieces(f_buf, f_z, fz_s, fz_r, f1_s, f1_r, f2_s, f2_r, fc_s, fc_r, f_first)
    rows_out[...] = rows.T.astype(BF16)
    squares[...] = jnp.zeros_like(squares)
    l_log[...] = jnp.zeros_like(l_log)
    f_log[...] = jnp.zeros_like(f_log)
    for j, t, s in others(NX, x):
        recv(cx.at[j], (c_s, c_r, (j,)), at_x(s))
    sx[...] = (mapped[:, x] + cx[0].astype(F32) + cx[1].astype(F32) + cx[2].astype(F32)).reshape(NZ, 8, COLS)
    for j, t, _ in others(NZ, z):
        send(sx.at[t], dz.at[j], (d_s, d_r, (j,)), at_z(t))
    forward(f_buf, f1_s, f1_r, f2_s, f2_r, fc_s, fc_r, f_first)
    base = hid[:, feat].astype(F32) + off[...].reshape(1, COLS) + sx[z]
    gain_part = 1.0 / regain[c]
    for j, _, s in others(NZ, z):
        recv(dz.at[j], (d_s, d_r, (j,)), at_z(s))
        base = base + dz[j]
    l_state[...] = base

    l_pack[...] = pack(base * gain_part)
    for j, t, _ in others(NZ, z):
        send(l_pack, l_z.at[z], (lz_s, lz_r, (j,)), at_z(t))
    l_z[z] = l_pack[...]
    load_u.wait()
    rest(f_buf, f2_s, f2_r, fc_s, fc_r, f_first)
    own_pieces(l_buf, l_z, lz_s, lz_r, l1_s, l1_r, l2_s, l2_r, lc_s, lc_r, l_first)
    own_logits(f_buf, f_log)
    forward(l_buf, l1_s, l1_r, l2_s, l2_r, lc_s, lc_r, l_first)
    sibling_logits(f_buf, f_log, fc_s, fc_r)
    rest(l_buf, l2_s, l2_r, lc_s, lc_r, l_first)
    own_logits(l_buf, l_log)
    sibling_logits(l_buf, l_log, lc_s, lc_r)

    place = lax.broadcasted_iota(jnp.int32, (32, 128), 1)

    def local(i, _):
        part = pl.ds(pl.multiple_of(i * 32, 32), 32)
        mean = jnp.sum(squares[part, :], axis=1, keepdims=True) / D
        inverse = lax.rsqrt(mean + EPSILON)
        inv_cols[part, :] = jnp.broadcast_to(inverse, (32, 128))
        a, b = l_log[part, :] * inverse, f_log[part, :]
        l_log[part, :] = a
        a_peak, b_peak = jnp.max(a, axis=1, keepdims=True), jnp.max(b, axis=1, keepdims=True)
        weight = jnp.exp(b - b_peak)
        found = [
            a_peak, jnp.sum(jnp.exp(a - a_peak), axis=1, keepdims=True), b_peak,
            jnp.sum(weight, axis=1, keepdims=True), jnp.sum(weight * (b - a), axis=1, keepdims=True),
        ]
        tile = jnp.zeros((32, 128), F32)
        for n, v in enumerate(found):
            tile = jnp.where(place == n, jnp.broadcast_to(v, (32, 128)), tile)
        cols[part, :] = tile
        return 0

    lax.fori_loop(0, 8, local, 0)
    st_core[7] = cols[...].T[:8]
    for j, t, _ in group:
        send(st_core.at[7], st_core.at[j], (tc_s, tc_r, (j,)), t)
    for j, _, s in group:
        recv(st_core.at[j], (tc_s, tc_r, (j,)), s)
    found = merge([st_core[j] for j in range(8)])
    for buf, n, me, at, ss, rs in ((st_x, NX, x, at_x, tx_s, tx_r), (st_z, NZ, z, at_z, tz_s, tz_r)):
        buf[n - 1] = found
        for j, t, _ in others(n, me):
            send(buf.at[n - 1], buf.at[j], (ss, rs, (j,)), at(t))
        for j, _, s in others(n, me):
            recv(buf.at[j], (ss, rs, (j,)), at(s))
        found = merge([buf[j] for j in range(n)])
    lens_total = found[0:1] + jnp.log(found[1:2])
    final_total = found[2:3] + jnp.log(found[3:4])
    apart = found[4:5] / found[3:4] + lens_total - final_total
    tall = jnp.concatenate([stack_rows([lens_total, final_total, apart]), jnp.zeros((120, 256), F32)], axis=0)
    cols[...] = tall.T
    mine = pl.ds(pl.multiple_of(half * 128 + x * 32 + quarter * 8, 8), 8)
    div[...] = jnp.broadcast_to(cols[mine, 2:3], (8, 128))

    def slopes(i, _):
        part = pl.ds(pl.multiple_of(i * 32, 32), 32)
        totals = cols[part, :]
        a = l_log[part, :]
        rounded = (jnp.exp(a - totals[:, 0:1]) - jnp.exp(f_log[part, :] - totals[:, 1:2])).astype(BF16)
        grad[part, :] = rounded
        slope = jnp.sum(rounded.astype(F32) * a, axis=1, keepdims=True)
        sl_cols[part, :] = jnp.broadcast_to(slope, (32, 128))
        return 0

    lax.fori_loop(0, 8, slopes, 0)

    def back(yy, kk):
        block = pl.ds(pl.multiple_of((yy * 2 + kk) * COLS, 128), COLS)
        return lax.dot_general(
            grad[...], u[block, :], (((1,), (1,)), ((), ())), preferred_element_type=F32
        ).reshape(2, NX, 32, COLS)

    def slope_send(buf, n, me, at, ss, rs):
        for j, t, _ in others(n, me):
            send(buf.at[n - 1], buf.at[j], (ss, rs, (j,)), at(t))

    def slope_sum(buf, n, me, at, ss, rs):
        total = buf[n - 1]
        for j, _, s in others(n, me):
            recv(buf.at[j], (ss, rs, (j,)), at(s))
            total = total + buf[j]
        return total

    over_y = (sl_y, NY, y, at_y, py_s, py_r)
    over_x = (sl_x, NX, x, at_x, px_s, px_r)
    over_z = (sl_z, NZ, z, at_z, pz_s, pz_r)
    sl_core[0] = sl_cols[...].T[:8]
    send(sl_core.at[0], sl_core.at[1], (pc_s, pc_r, ()), sibling)

    def block_y(i):
        return lax.rem(y + 1 + i, NY)

    def hand_over(i):
        return copy(c_send.at[i], c_recv.at[i], gc_s.at[i], gc_r.at[i], sibling)

    def y_first(i):
        return copy(acc.at[i, 0], ry0.at[i], gy_s.at[i], gy_r.at[i], at_y(block_y(i)))

    def x_first(i, j, t):
        return copy(acc.at[i, 1, t], rx1.at[j, i], gx_s.at[j, i], gx_r.at[j, i], at_x(t))

    def away(i):
        c_send[i] = back(block_y(i), 1 - k)
        hand_over(i).start()

    away(0)

    def home(i, _):
        @pl.when(i < NY - 1)
        def _():
            away(i + 1)

        acc[i] = back(block_y(i), k)
        hand_over(i).wait_recv()
        acc[i] += c_recv[i]

        @pl.when(i < NY - 1)
        def _():
            y_first(i).start()

        for j, t, _ in others(NX, x):
            x_first(i, j, t).start()
        return 0

    lax.fori_loop(0, NY, home, 0)
    recv(sl_core.at[1], (pc_s, pc_r, ()), sibling)
    sl_y[NY - 1] = sl_core[0] + sl_core[1]
    slope_send(*over_y)
    for i in range(NY - 1):
        y_first(i).wait_recv()

    def add0(i, _):
        r0[i] = acc[NY - 1, 0, i] + ry0[0, i] + ry0[1, i] + ry0[2, i]
        return 0

    lax.fori_loop(0, NX, add0, 0)
    for j, t, _ in others(NX, x):
        send(r0.at[t], rx0.at[j], (g2_s, g2_r, (0, j)), at_x(t))
    sl_x[NX - 1] = slope_sum(*over_y)
    slope_send(*over_x)

    for i in range(NY):
        for j, t, _ in others(NX, x):
            x_first(i, j, t).wait_recv()
        r1[i] = acc[i, 1, x] + rx1[0, i] + rx1[1, i] + rx1[2, i]
        if i < NY - 1:
            send(r1.at[i], ry1.at[i], (g2_s, g2_r, (1, i)), at_y(block_y(i)))
    for j, _, s in others(NX, x):
        recv(rx0.at[j], (g2_s, g2_r, (0, j)), at_x(s))
    for i in range(NY - 1):
        recv(ry1.at[i], (g2_s, g2_r, (1, i)), at_y(block_y(i)))
    sz[0:4] = (r0[x] + rx0[0] + rx0[1] + rx0[2]).reshape(4, 8, COLS)
    sz[4:8] = (r1[NY - 1] + ry1[0] + ry1[1] + ry1[2]).reshape(4, 8, COLS)
    for j, t, _ in others(NZ, z):
        send(sz.at[t], rz.at[j], (gz_s, gz_r, (j,)), at_z(t))
    sl_z[NZ - 1] = slope_sum(*over_x)
    slope_send(*over_z)
    state_grad = sz[z]
    for j, _, s in others(NZ, z):
        recv(rz.at[j], (gz_s, gz_r, (j,)), at_z(s))
        state_grad = state_grad + rz[j]
    cols[...] = jnp.concatenate([slope_sum(*over_z), jnp.zeros((120, 256), F32)], axis=0).T
    inverse = inv_cols[mine, 0:1]
    slope = cols[mine, 0:1] / D
    delta = inverse * (gain_part * state_grad) - l_state[...] * (inverse * inverse * slope)
    sd_z[mine8] = pack(delta)
    own = sd_z.at[mine8]
    for j, t, _ in others(NZ, z):
        send(own, own, (oz_s, oz_r, (j,)), at_z(t))
    for j, t, _ in others(NX, x):
        send(own, own, (ox_s, ox_r, (0, j)), at_x(t))
    for q, _, s in others(NZ, z):
        piece = sd_z.at[slot_of(s, x)]
        recv(piece, (oz_s, oz_r, (q,)), at_z(s))
        for j, t, _ in others(NX, x):
            send(piece, piece, (ox_s, ox_r, (q + 1, j)), at_x(t))
    for q in range(NZ):
        for j, _, s in others(NX, x):
            piece = sd_z.at[slot_of(lax.rem(z + (NZ - q), NZ), s)]
            recv(piece, (ox_s, ox_r, (q, j)), at_x(s))
    found = sd_z[...].astype(F32)
    sd_out[...] = jnp.concatenate([found[:, :8], found[:, 8:, :384]], axis=2).reshape(256, COLS).astype(BF16)

    for i in range(NY):
        hand_over(i).wait_send()
        if i < NY - 1:
            y_first(i).wait_send()
        for j, t, _ in others(NX, x):
            x_first(i, j, t).wait_send()
    for one in unsent:
        one.wait_send()


def finish(rows, delta, div, gt, goff, divergence):
    gt[...] = jnp.dot(rows[...], delta[...], preferred_element_type=F32)[:ROWS]
    goff[...] = jnp.sum(delta[...].astype(F32), axis=0)
    divergence[...] = div[...].T[0]


def on_device(hidden, final_hidden, translator, offset, norm_gain, unembed):
    vm = pltpu.VMEM
    dma = pltpu.SemaphoreType.DMA
    blocks = [
        vm((D, VOC), BF16), vm((32, 16, 128), BF16), vm((32, 16, 128), BF16), vm((256, COLS), BF16),
        vm((2, NX, 32, COLS), F32), vm((2, NX, 32, COLS), BF16), vm((3, 2, 32, COLS), BF16),
        vm((NZ, 8, COLS), F32), vm((7, 8, COLS), F32),
        vm((8, D), F32), vm((16, 512), BF16), vm((NZ, 16, 512), BF16), vm((2, NY, 2, NX, 32, COLS), BF16),
        vm((16, 512), BF16), vm((NZ, 16, 512), BF16), vm((2, NY, 2, NX, 32, COLS), BF16), vm((8, COLS), F32),
        vm((8, 8, COLS), F32), vm((256, 128), F32),
        vm((256, VOC), F32), vm((256, VOC), F32),
        vm((8, 8, 256), F32), vm((NX, 8, 256), F32), vm((NZ, 8, 256), F32),
        vm((2, 8, 256), F32), vm((NY, 8, 256), F32), vm((NX, 8, 256), F32), vm((NZ, 8, 256), F32),
        vm((256, 128), F32), vm((256, 128), F32), vm((256, 128), F32), vm((256, VOC), BF16),
        vm((NY, 2, NX, 32, COLS), F32), vm((NY, 2, NX, 32, COLS), F32), vm((NY, 2, NX, 32, COLS), F32),
        vm((3, NX, 32, COLS), F32), vm((3, NY, 32, COLS), F32), vm((NX, 32, COLS), F32), vm((NY, 32, COLS), F32),
        vm((3, 32, COLS), F32), vm((3, 32, COLS), F32), vm((NZ, 8, COLS), F32), vm((7, 8, COLS), F32),
        vm((32, 16, 512), BF16),
    ]
    pairs = [
        (31,), (3,), (7,),
        (7,), (2, 3), (2, 4, 3), (2, 4, 4),
        (7,), (2, 3), (2, 4, 3), (2, 4, 4),
        (7,), (3,), (7,),
        (), (3,), (3,), (7,),
        (4,), (3,), (3, 4), (2, 3), (7,),
        (7,), (8, 3),
    ]
    sems = [dma]
    for shape in pairs:
        sems += [dma(shape) if shape else dma] * 2
    whole = pl.BlockSpec(memory_space=pltpu.VMEM)
    rows, delta, div = pl.pallas_call(
        kernel,
        out_shape=(
            jax.ShapeDtypeStruct((256, 256), BF16),
            jax.ShapeDtypeStruct((256, COLS), BF16),
            jax.ShapeDtypeStruct((8, 128), F32),
        ),
        in_specs=[whole] * 5 + [pl.BlockSpec(memory_space=pl.ANY)],
        out_specs=(whole, whole, whole),
        scratch_shapes=blocks + sems,
        compiler_params=pltpu.CompilerParams(
            collective_id=0, has_side_effects=True, vmem_limit_bytes=56 * 2**20
        ),
        name="lens_step",
    )(hidden, final_hidden, translator, offset, norm_gain, unembed)
    return pl.pallas_call(
        finish,
        out_shape=(
            jax.ShapeDtypeStruct((ROWS, COLS), F32),
            jax.ShapeDtypeStruct((COLS,), F32),
            jax.ShapeDtypeStruct((8,), F32),
        ),
        in_specs=[whole] * 3,
        out_specs=(whole, whole, whole),
        name="finish",
    )(rows, delta, div)


def solution(mesh):
    placed = (P("dp", None), P("dp", None), P("dp", "vocab"), P("vocab"), P(), P(None, ("dp", "vocab")))
    return jax.shard_map(
        on_device,
        mesh=mesh,
        in_specs=placed,
        out_specs=(P("dp", "vocab"), P("vocab"), P("dp")),
        check_vma=False,
    )
```

time: 159 us -> 140 us (0.88)
  Pallas kernels: 150 us -> 138 us
  local copies, waits for them, and re-layouts: 5.98 us -> 0 us
    pallas_call x1 -> x2, Pallas kernels: 150 us -> 138 us  [the longest x1 136 us: on_device(): pl.pallas_call(kernel, out_shape=(jax.ShapeDtypeStruct((256, 256), BF16),...]
    reshape x2 -> x0, local copies, waits for them, and re-layouts: 2.6 us -> none  [the longest x1 1.34 us: on_device(): norm_gain.reshape(1, D)]
    unnamed x1 -> x0, local copies, waits for them, and re-layouts: 2.07 us -> none
where the time goes in v2:
time: 140 us; the launch traced here: 139 us
  Pallas kernels  138 us (99%)
    pallas_call x1, Pallas kernels, on_device(): pl.pallas_call(kernel, out_shape=(jax.ShapeDtypeStruct((256, 256), BF16),...  136 us

profile of v2, /device:TPU:1, one launch (start us, length us, event | category | flops | bytes accessed | tf_op | source)
XLA Modules:
  0.0 138.9 jit_solution(9464880171102868668)
XLA Ops:
  0.6 136.0 %lens_step.1 = (bf16[256,256]{1,0:T(8,128)(2,1)}, bf16[256,896]{1,0:T(8,128)(2,1)}, f32[8,128]{1,0:T(8,128)}) custom-call(bf16[8,7168]{1,0:T(8,128)(2,1)} %hid.1, bf16[8,7168]{1,0:T(8,128)(2,1)} %fin.1, bf16[224,896]{1,0:T(8,128)(2,1)} %tw.1, f32[896]{0:T(1024)} %off.1, bf16[7168]{0:T(1024)(128)(2,1)} %gain.1, bf16[7168,512]{1,0:T(8,128)(2,1)} %unemb.1), custom_call_target="tpu_custom_call" | custom-call | tf_op jit(solution)/shard_map/lens_step/pallas_call | solution.py:486
  136.6 2.2 %finish.1 = (f32[224,896]{1,0:T(8,128)}, f32[896]{0:T(1024)}, f32[8]{0:T(128)}) custom-call(bf16[256,256]{1,0:T(8,128)(2,1)} %get-tuple-element.6.rows, bf16[256,896]{1,0:T(8,128)(2,1)} %get-tuple-element.7.delta, f32[8,128]{1,0:T(8,128)} %get-tuple-element.8.div), custom_call_target="tpu_custom_call" | custom-call | tf_op jit(solution)/shard_map/finish/pallas_call | solution.py:501

commit v3 on v2

--- a/solution.py
+++ b/solution.py
@@ -46,18 +46,18 @@
 
 
 def kernel(
-    hid, fin, tw, off, gain, unemb, rows_out, sd_out, div,
-    u, hpack, hin, twp, mapped, mapped_b, cx, sx, dz,
-    f_norm, f_pack, f_z, f_buf, l_pack, l_z, l_buf, l_state, regain, squares,
+    hid_in, fin_in, tw_in, off_in, gain_in, unemb, rows_out, sd_out, div,
+    hid, fin, off, gain, u, hpack, hin, twp, mapped, mapped_b, cx, sx, dz,
+    f_norm, f_pack, f_z, f_buf, l_pack, l_z, l_buf, l_state, gains, regain, squares,
     l_log, f_log, st_core, st_x, st_z, sl_core, sl_y, sl_x, sl_z, cols, inv_cols, sl_cols, grad,
-    c_send, c_recv, acc, ry0, rx1, r0, r1, rx0, ry1, sz, rz,
+    c_send, c_recv, acc, fy, ry, fx, rx, r0, r1, rx0, ry1, sz, rz,
     sd_z,
-    u_sem, a_s, a_r, c_s, c_r, d_s, d_r,
+    in_sem, a_s, a_r, c_s, c_r, d_s, d_r,
     fz_s, fz_r, f1_s, f1_r, f2_s, f2_r, fc_s, fc_r,
     lz_s, lz_r, l1_s, l1_r, l2_s, l2_r, lc_s, lc_r,
     tc_s, tc_r, tx_s, tx_r, tz_s, tz_r,
     pc_s, pc_r, py_s, py_r, px_s, px_r, pz_s, pz_r,
-    gc_s, gc_r, gy_s, gy_r, gx_s, gx_r, g2_s, g2_r, gz_s, gz_r,
+    gc_s, gc_r, yf_s, yf_r, yn_s, yn_r, xf_s, xf_r, xn_s, xn_r, xs_s, xs_r, g2_s, g2_r, gz_s, gz_r,
     oz_s, oz_r, ox_s, ox_r,
 ):
     r, c = lax.axis_index("dp"), lax.axis_index("vocab")
@@ -114,52 +114,57 @@
     partners += [t for _, t, _ in group]
     for p in partners:
         pl.semaphore_signal(barrier, inc=1, device_id=p, device_id_type=MESH)
-    load_u = pltpu.make_async_copy(unemb, u, u_sem)
-    load_u.start()
+    pairs = [(hid_in, hid), (fin_in, fin), (gain_in, gain), (tw_in, twp.at[pl.ds(0, ROWS)]), (off_in, off), (unemb, u)]
+    loads = [pltpu.make_async_copy(src, dst, in_sem.at[i]) for i, (src, dst) in enumerate(pairs)]
+    load_hid, load_fin, load_gain, load_tw, load_off, load_u = loads
+    for load in loads:
+        load.start()
+    load_hid.wait()
 
     flat = hid[...].astype(F32)
     for i in range(NZ * NX):
         low = jnp.concatenate([flat[:, i * ROWS + 128 : (i + 1) * ROWS], jnp.zeros((8, 32), F32)], axis=1)
         hpack[i] = jnp.concatenate([flat[:, i * ROWS : i * ROWS + 128], low], axis=0).astype(BF16)
+    pl.semaphore_wait(barrier, len(partners))
+
+    mine8 = slot_of(z, x)
+    for j, (zz, xx), _ in plane:
+        send(hpack.at[zz * NX + xx], hin.at[mine8], (a_s, a_r, (j,)), (zz * NX + xx, c))
+    hin[mine8] = hpack[r]
+    load_fin.wait()
+    load_gain.wait()
     wide = fin[...].astype(F32)
     final_inverse = lax.rsqrt(jnp.sum(wide * wide, axis=1, keepdims=True) / D + EPSILON)
     gain_all = gain[...].astype(F32).reshape(1, D)
     f_norm[...] = wide * final_inverse * gain_all
     f_pack[...] = pack(f_norm[:, feat])
     for i in range(8):
-        regain[i] = jnp.broadcast_to(1.0 / gain_all[:, i * COLS : (i + 1) * COLS], (8, COLS))
-    twp[:ROWS] = tw[...]
+        gains[i] = jnp.broadcast_to(gain_all[:, i * COLS : (i + 1) * COLS], (8, COLS))
+        regain[i] = 1.0 / gains[i]
     twp[ROWS:] = jnp.zeros((256 - ROWS, COLS), BF16)
-    pl.semaphore_wait(barrier, len(partners))
-
-    mine8 = slot_of(z, x)
-    for j, (zz, xx), _ in plane:
-        send(hpack.at[zz * NX + xx], hin.at[mine8], (a_s, a_r, (j,)), (zz * NX + xx, c))
     for j, t, _ in others(NZ, z):
         send(f_pack, f_z.at[z], (fz_s, fz_r, (j,)), at_z(t))
-    hin[mine8] = hpack[r]
     f_z[z] = f_pack[...]
 
-    f_first, l_first = ("x", "x"), ("x", "y")
-
-    def own_pieces(buf, zbuf, zs, zr, s1, r1, s2, r2, sc, rc, firsts):
-        for j, _, s in others(NZ, z):
-            recv(zbuf.at[s], (zs, zr, (j,)), at_z(s))
-        flat = unpack(zbuf[...])
+    f_first, l_first = ("x", "y"), ("x", "y")
+
+    def own_pieces(buf, flat, s1, r1, s2, r2, sc, rc, firsts):
         for h in range(2):
             buf[k, y, h, x] = flat[h * 32 : (h + 1) * 32]
-        for h, first in enumerate(firsts):
+        for stage in range(2):
+            for h, first in enumerate(firsts):
+                piece = buf.at[k, y, h, x]
+                along_x = (first == "x") == (stage == 0)
+                n, me, at = (NX, x, at_x) if along_x else (NY, y, at_y)
+                for j, t, _ in others(n, me):
+                    sem = (s1, r1, (h, j)) if stage == 0 else (s2, r2, (h, 0, j))
+                    send(piece, piece, sem, at(t))
+        for h in range(2):
             piece = buf.at[k, y, h, x]
-            ways = [(NX, x, at_x), (NY, y, at_y)]
-            (n1, m1, at1), (n2, m2, at2) = ways if first == "x" else ways[::-1]
-            for j, t, _ in others(n1, m1):
-                send(piece, piece, (s1, r1, (h, j)), at1(t))
-            for j, t, _ in others(n2, m2):
-                send(piece, piece, (s2, r2, (h, 0, j)), at2(t))
             send(piece, piece, (sc, rc, (h, 0, 0)), sibling)
 
     def forward(buf, s1, r1, s2, r2, sc, rc, firsts):
-        for q in range(1, 4):
+        for q in (1, 3, 2):
             for h, first in enumerate(firsts):
                 if first == "x":
                     s = lax.rem(x + (NX - q), NX)
@@ -174,9 +179,9 @@
                     send(piece, piece, (s2, r2, (h, q, j)), at2(t))
                 send(piece, piece, (sc, rc, slot), sibling)
 
-    def rest(buf, s2, r2, sc, rc, firsts, each=lambda q: None):
-        for q in range(1, 4):
-            for j in range(4):
+    def rest(buf, s2, r2, sc, rc, firsts):
+        for j in (0, 1, 3, 2):
+            for q in (1, 3, 2):
                 for h, first in enumerate(firsts):
                     if first == "x":
                         yy, xx = lax.rem(y + (NY - q), NY), lax.rem(x + (NX - j), NX)
@@ -187,63 +192,74 @@
                     piece = buf.at[k, yy, h, xx]
                     recv(piece, (s2, r2, (h, j, q - 1)), dev)
                     send(piece, piece, (sc, rc, slot), sibling)
-            each(q)
-
-    def logits(buf, log, kk, yy):
-        cc = yy * 2 + kk
-        block = pl.ds(pl.multiple_of(cc * COLS, 128), COLS)
-        value = buf[kk, yy].reshape(256, COLS)
-        log[...] += jnp.dot(value, u[block, :], preferred_element_type=F32)
-        if buf is l_buf:
-            scale = regain[cc][0:1]
-            total = squares[...]
-            for i in range(COLS // 128):
-                lanes = slice(i * 128, (i + 1) * 128)
-                plain = value[:, lanes].astype(F32) * scale[:, lanes]
-                total = total + plain * plain
-            squares[...] = total
-
-    def own_logits(buf, log):
-        def step(q, _):
-            logits(buf, log, k, lax.rem(y + (NY - q), NY))
+
+    def all_logits(buf, log, sc, rc):
+        def step(n, _):
+            q = lax.rem(n, NY)
+            yy, kk = lax.rem(y + (NY - q), NY), jnp.where(n < NY, k, 1 - k)
+
+            @pl.when(n >= NY)
+            def _():
+                for h in range(2):
+                    for j in range(4):
+                        xx = lax.rem(x + (NX - j), NX)
+                        recv(buf.at[1 - k, yy, h, xx], (sc, rc, (h, q, j)), sibling)
+
+            cc = yy * 2 + kk
+            block = pl.ds(pl.multiple_of(cc * COLS, 128), COLS)
+            value = buf[kk, yy].reshape(256, COLS)
+            log[...] += jnp.dot(value, u[block, :], preferred_element_type=F32)
+            if buf is l_buf:
+                scale = regain[cc][0:1]
+                total = squares[...]
+                for i in range(COLS // 128):
+                    lanes = slice(i * 128, (i + 1) * 128)
+                    plain = value[:, lanes].astype(F32) * scale[:, lanes]
+                    total = total + plain * plain
+                squares[...] = total
             return 0
 
-        lax.fori_loop(0, NY, step, 0)
-
-    def sibling_logits(buf, log, sc, rc):
-        def step(q, _):
-            yy = lax.rem(y + (NY - q), NY)
-            for h in range(2):
-                for j in range(4):
-                    xx = lax.rem(x + (NX - j), NX)
-                    recv(buf.at[1 - k, yy, h, xx], (sc, rc, (h, q, j)), sibling)
-            logits(buf, log, 1 - k, yy)
-            return 0
-
-        lax.fori_loop(0, NY, step, 0)
+        lax.fori_loop(0, 8, step, 0)
 
     for j, _, (zz, xx) in plane:
         recv(hin.at[slot_of(zz, xx)], (a_s, a_r, (j,)), (zz * NX + xx, c))
     found = hin[...].astype(F32)
+    load_tw.wait()
     rows = jnp.concatenate([found[:, :8].reshape(256, 128), found[:, 8:].reshape(256, 128)], axis=1)
     product = jnp.dot(rows.astype(BF16), twp[...], preferred_element_type=F32)
     mapped[...] = product.reshape(2, NX, 32, COLS)
     mapped_b[...] = product.astype(BF16).reshape(2, NX, 32, COLS)
-    for j, t, _ in others(NX, x):
-        send(mapped_b.at[:, t], cx.at[j], (c_s, c_r, (j,)), at_x(t))
-    own_pieces(f_buf, f_z, fz_s, fz_r, f1_s, f1_r, f2_s, f2_r, fc_s, fc_r, f_first)
+    quarters = [(h, pl.ds(16 * p, 16)) for h in range(2) for p in range(2)]
+    for p, (h, part) in enumerate(quarters):
+        for j, t, _ in others(NX, x):
+            send(mapped_b.at[h, t, part], cx.at[j, h, part], (c_s, c_r, (p, j)), at_x(t))
+
+    def z_sum(src, dst, ss, rs, zz):
+        place = lax.rem(zz - z + NZ, NZ) - 1
+        return copy(src.at[zz], dst.at[place], ss.at[place], rs.at[place], at_z(zz))
+
+    def z_send(src, dst, ss, rs, zz):
+        @pl.when(z != zz)
+        def _():
+            z_sum(src, dst, ss, rs, zz).start()
+
+    for j, _, s in others(NZ, z):
+        recv(f_z.at[s], (fz_s, fz_r, (j,)), at_z(s))
+    own_pieces(f_buf, unpack(f_z[...]), f1_s, f1_r, f2_s, f2_r, fc_s, fc_r, f_first)
     rows_out[...] = rows.T.astype(BF16)
-    squares[...] = jnp.zeros_like(squares)
-    l_log[...] = jnp.zeros_like(l_log)
-    f_log[...] = jnp.zeros_like(f_log)
-    for j, t, s in others(NX, x):
-        recv(cx.at[j], (c_s, c_r, (j,)), at_x(s))
-    sx[...] = (mapped[:, x] + cx[0].astype(F32) + cx[1].astype(F32) + cx[2].astype(F32)).reshape(NZ, 8, COLS)
-    for j, t, _ in others(NZ, z):
-        send(sx.at[t], dz.at[j], (d_s, d_r, (j,)), at_z(t))
+    for p, (h, part) in enumerate(quarters):
+        for j, _, s in others(NX, x):
+            recv(cx.at[j, h, part], (c_s, c_r, (p, j)), at_x(s))
+        total = mapped[h, x, part]
+        for j in range(3):
+            total = total + cx[j, h, part].astype(F32)
+        sx[2 * p : 2 * p + 2] = total.reshape(2, 8, COLS)
+        z_send(sx, dz, d_s, d_r, 2 * p)
+        z_send(sx, dz, d_s, d_r, 2 * p + 1)
+    load_off.wait()
     forward(f_buf, f1_s, f1_r, f2_s, f2_r, fc_s, fc_r, f_first)
     base = hid[:, feat].astype(F32) + off[...].reshape(1, COLS) + sx[z]
-    gain_part = 1.0 / regain[c]
+    gain_part = gains[c]
     for j, _, s in others(NZ, z):
         recv(dz.at[j], (d_s, d_r, (j,)), at_z(s))
         base = base + dz[j]
@@ -253,15 +269,18 @@
     for j, t, _ in others(NZ, z):
         send(l_pack, l_z.at[z], (lz_s, lz_r, (j,)), at_z(t))
     l_z[z] = l_pack[...]
+    squares[...] = jnp.zeros_like(squares)
+    l_log[...] = jnp.zeros_like(l_log)
+    f_log[...] = jnp.zeros_like(f_log)
+    for j, _, s in others(NZ, z):
+        recv(l_z.at[s], (lz_s, lz_r, (j,)), at_z(s))
+    own_pieces(l_buf, unpack(l_z[...]), l1_s, l1_r, l2_s, l2_r, lc_s, lc_r, l_first)
+    forward(l_buf, l1_s, l1_r, l2_s, l2_r, lc_s, lc_r, l_first)
+    rest(f_buf, f2_s, f2_r, fc_s, fc_r, f_first)
     load_u.wait()
-    rest(f_buf, f2_s, f2_r, fc_s, fc_r, f_first)
-    own_pieces(l_buf, l_z, lz_s, lz_r, l1_s, l1_r, l2_s, l2_r, lc_s, lc_r, l_first)
-    own_logits(f_buf, f_log)
-    forward(l_buf, l1_s, l1_r, l2_s, l2_r, lc_s, lc_r, l_first)
-    sibling_logits(f_buf, f_log, fc_s, fc_r)
+    all_logits(f_buf, f_log, fc_s, fc_r)
     rest(l_buf, l2_s, l2_r, lc_s, lc_r, l_first)
-    own_logits(l_buf, l_log)
-    sibling_logits(l_buf, l_log, lc_s, lc_r)
+    all_logits(l_buf, l_log, lc_s, lc_r)
 
     place = lax.broadcasted_iota(jnp.int32, (32, 128), 1)
 
@@ -347,66 +366,115 @@
     def hand_over(i):
         return copy(c_send.at[i], c_recv.at[i], gc_s.at[i], gc_r.at[i], sibling)
 
-    def y_first(i):
-        return copy(acc.at[i, 0], ry0.at[i], gy_s.at[i], gy_r.at[i], at_y(block_y(i)))
-
-    def x_first(i, j, t):
-        return copy(acc.at[i, 1, t], rx1.at[j, i], gx_s.at[j, i], gx_r.at[j, i], at_x(t))
+    def y_far(p):
+        return copy(acc.at[1, 0, pl.ds(2 * p, 2)], fy.at[p], yf_s.at[p], yf_r.at[p], at_y(block_y(2 * p)))
+
+    def y_near(p, part):
+        two = pl.ds(2 * part, 2)
+        sem = (yn_s.at[p, part], yn_r.at[p, part])
+        return copy(acc.at[2 * p, 0, two], ry.at[p, two], *sem, at_y(block_y(2 * p)))
+
+    def beside(i, far):
+        return lax.div(i, 2) if far else 1 - lax.div(i, 2)
+
+    def x_at(way):
+        return lax.rem(x + 1 + 2 * way, NX)
+
+    def x_far(i):
+        way = beside(i, True)
+        return copy(acc.at[i, 1, lax.rem(x + 2, NX)], fx.at[i], xf_s.at[i], xf_r.at[i], at_x(x_at(way)))
+
+    def x_near(i):
+        way = beside(i, False)
+        return copy(acc.at[i, 1, x_at(way)], rx.at[way, i], xn_s.at[i], xn_r.at[i], at_x(x_at(way)))
+
+    def x_sum(i):
+        way = beside(i, True)
+        return copy(acc.at[i, 1, x_at(way)], rx.at[way, i], xs_s.at[i], xs_r.at[i], at_x(x_at(way)))
 
     def away(i):
         c_send[i] = back(block_y(i), 1 - k)
         hand_over(i).start()
 
-    away(0)
-
-    def home(i, _):
-        @pl.when(i < NY - 1)
-        def _():
-            away(i + 1)
-
+    def order(i):
+        return jnp.where(i < 2, 1 - i, i)
+
+    def home(i, n):
         acc[i] = back(block_y(i), k)
         hand_over(i).wait_recv()
         acc[i] += c_recv[i]
 
-        @pl.when(i < NY - 1)
+        @pl.when(n == 0)
         def _():
-            y_first(i).start()
-
-        for j, t, _ in others(NX, x):
-            x_first(i, j, t).start()
+            y_far(0).start()
+            y_far(1).start()
+
+        @pl.when(n == 1)
+        def _():
+            y_near(0, 1).start()
+
+        @pl.when(n == 2)
+        def _():
+            y_near(1, 0).start()
+
+        x_far(i).start()
+        x_near(i).start()
+
+    def both(n, _):
+        @pl.when(n < NY)
+        def _():
+            away(order(n))
+
+        @pl.when(n > 0)
+        def _():
+            home(order(n - 1), n - 1)
+
         return 0
 
-    lax.fori_loop(0, NY, home, 0)
+    lax.fori_loop(0, NY + 1, both, 0)
     recv(sl_core.at[1], (pc_s, pc_r, ()), sibling)
     sl_y[NY - 1] = sl_core[0] + sl_core[1]
     slope_send(*over_y)
-    for i in range(NY - 1):
-        y_first(i).wait_recv()
+    for p in range(2):
+        y_far(p).wait_recv()
+        acc[2 * p, 0, 2 * p : 2 * p + 2] += fy[p]
+        y_near(p, p).start()
+    for i in (1, 0, 2, 3):
+        x_far(i).wait_recv()
+        acc[i, 1, x_at(beside(i, True))] += fx[i]
+        x_sum(i).start()
+    for p in range(2):
+        for part in range(2):
+            y_near(p, part).wait_recv()
 
     def add0(i, _):
-        r0[i] = acc[NY - 1, 0, i] + ry0[0, i] + ry0[1, i] + ry0[2, i]
+        r0[i] = acc[NY - 1, 0, i] + ry[0, i] + ry[1, i]
         return 0
 
     lax.fori_loop(0, NX, add0, 0)
-    for j, t, _ in others(NX, x):
-        send(r0.at[t], rx0.at[j], (g2_s, g2_r, (0, j)), at_x(t))
+    eights = [pl.ds(8 * q, 8) for q in range(4)]
+    for q, part in enumerate(eights):
+        for j, t, _ in others(NX, x):
+            send(r0.at[t, part], rx0.at[j, part], (g2_s, g2_r, (0, j, q)), at_x(t))
     sl_x[NX - 1] = slope_sum(*over_y)
     slope_send(*over_x)
 
     for i in range(NY):
-        for j, t, _ in others(NX, x):
-            x_first(i, j, t).wait_recv()
-        r1[i] = acc[i, 1, x] + rx1[0, i] + rx1[1, i] + rx1[2, i]
-        if i < NY - 1:
-            send(r1.at[i], ry1.at[i], (g2_s, g2_r, (1, i)), at_y(block_y(i)))
-    for j, _, s in others(NX, x):
-        recv(rx0.at[j], (g2_s, g2_r, (0, j)), at_x(s))
-    for i in range(NY - 1):
-        recv(ry1.at[i], (g2_s, g2_r, (1, i)), at_y(block_y(i)))
-    sz[0:4] = (r0[x] + rx0[0] + rx0[1] + rx0[2]).reshape(4, 8, COLS)
-    sz[4:8] = (r1[NY - 1] + ry1[0] + ry1[1] + ry1[2]).reshape(4, 8, COLS)
-    for j, t, _ in others(NZ, z):
-        send(sz.at[t], rz.at[j], (gz_s, gz_r, (j,)), at_z(t))
+        x_near(i).wait_recv()
+        x_sum(i).wait_recv()
+        r1[i] = acc[i, 1, x] + rx[0, i] + rx[1, i]
+    for q, part in enumerate(eights):
+        for i in range(NY - 1):
+            send(r1.at[i, part], ry1.at[i, part], (g2_s, g2_r, (1, i, q)), at_y(block_y(i)))
+    for q, part in enumerate(eights):
+        for j, _, s in others(NX, x):
+            recv(rx0.at[j, part], (g2_s, g2_r, (0, j, q)), at_x(s))
+        sz[q] = r0[x, part] + rx0[0, part] + rx0[1, part] + rx0[2, part]
+        z_send(sz, rz, gz_s, gz_r, q)
+        for i in range(NY - 1):
+            recv(ry1.at[i, part], (g2_s, g2_r, (1, i, q)), at_y(block_y(i)))
+        sz[4 + q] = r1[NY - 1, part] + ry1[0, part] + ry1[1, part] + ry1[2, part]
+        z_send(sz, rz, gz_s, gz_r, 4 + q)
     sl_z[NZ - 1] = slope_sum(*over_x)
     slope_send(*over_z)
     state_grad = sz[z]
@@ -437,10 +505,16 @@
 
     for i in range(NY):
         hand_over(i).wait_send()
-        if i < NY - 1:
-            y_first(i).wait_send()
-        for j, t, _ in others(NX, x):
-            x_first(i, j, t).wait_send()
+        x_far(i).wait_send()
+        x_near(i).wait_send()
+        x_sum(i).wait_send()
+    for p in range(2):
+        y_far(p).wait_send()
+        for part in range(2):
+            y_near(p, part).wait_send()
+    for _, t, _ in others(NZ, z):
+        z_sum(sx, dz, d_s, d_r, t).wait_send()
+        z_sum(sz, rz, gz_s, gz_r, t).wait_send()
     for one in unsent:
         one.wait_send()
 
@@ -455,31 +529,33 @@
     vm = pltpu.VMEM
     dma = pltpu.SemaphoreType.DMA
     blocks = [
+        vm((8, D), BF16), vm((8, D), BF16), vm((COLS,), F32), vm((D,), BF16),
         vm((D, VOC), BF16), vm((32, 16, 128), BF16), vm((32, 16, 128), BF16), vm((256, COLS), BF16),
         vm((2, NX, 32, COLS), F32), vm((2, NX, 32, COLS), BF16), vm((3, 2, 32, COLS), BF16),
         vm((NZ, 8, COLS), F32), vm((7, 8, COLS), F32),
         vm((8, D), F32), vm((16, 512), BF16), vm((NZ, 16, 512), BF16), vm((2, NY, 2, NX, 32, COLS), BF16),
         vm((16, 512), BF16), vm((NZ, 16, 512), BF16), vm((2, NY, 2, NX, 32, COLS), BF16), vm((8, COLS), F32),
-        vm((8, 8, COLS), F32), vm((256, 128), F32),
+        vm((8, 8, COLS), F32), vm((8, 8, COLS), F32), vm((256, 128), F32),
         vm((256, VOC), F32), vm((256, VOC), F32),
         vm((8, 8, 256), F32), vm((NX, 8, 256), F32), vm((NZ, 8, 256), F32),
         vm((2, 8, 256), F32), vm((NY, 8, 256), F32), vm((NX, 8, 256), F32), vm((NZ, 8, 256), F32),
         vm((256, 128), F32), vm((256, 128), F32), vm((256, 128), F32), vm((256, VOC), BF16),
         vm((NY, 2, NX, 32, COLS), F32), vm((NY, 2, NX, 32, COLS), F32), vm((NY, 2, NX, 32, COLS), F32),
-        vm((3, NX, 32, COLS), F32), vm((3, NY, 32, COLS), F32), vm((NX, 32, COLS), F32), vm((NY, 32, COLS), F32),
+        vm((2, 2, 32, COLS), F32), vm((2, NX, 32, COLS), F32), vm((NY, 32, COLS), F32), vm((2, NY, 32, COLS), F32),
+        vm((NX, 32, COLS), F32), vm((NY, 32, COLS), F32),
         vm((3, 32, COLS), F32), vm((3, 32, COLS), F32), vm((NZ, 8, COLS), F32), vm((7, 8, COLS), F32),
         vm((32, 16, 512), BF16),
     ]
     pairs = [
-        (31,), (3,), (7,),
+        (31,), (4, 3), (7,),
         (7,), (2, 3), (2, 4, 3), (2, 4, 4),
         (7,), (2, 3), (2, 4, 3), (2, 4, 4),
         (7,), (3,), (7,),
         (), (3,), (3,), (7,),
-        (4,), (3,), (3, 4), (2, 3), (7,),
+        (4,), (2,), (2, 2), (4,), (4,), (4,), (2, 3, 4), (7,),
         (7,), (8, 3),
     ]
-    sems = [dma]
+    sems = [dma((6,))]
     for shape in pairs:
         sems += [dma(shape) if shape else dma] * 2
     whole = pl.BlockSpec(memory_space=pltpu.VMEM)
@@ -490,7 +566,7 @@
             jax.ShapeDtypeStruct((256, COLS), BF16),
             jax.ShapeDtypeStruct((8, 128), F32),
         ),
-        in_specs=[whole] * 5 + [pl.BlockSpec(memory_space=pl.ANY)],
+        in_specs=[pl.BlockSpec(memory_space=pl.ANY)] * 6,
         out_specs=(whole, whole, whole),
         scratch_shapes=blocks + sems,
         compiler_params=pltpu.CompilerParams(

time: 140 us -> 124 us (0.89)
  Pallas kernels: 138 us -> 123 us
    pallas_call x1, Pallas kernels: 136 us -> 121 us  [on_device(): pl.pallas_call(kernel, out_shape=(jax.ShapeDtypeStruct((256, 256), BF16),...]
where the time goes in v3:
time: 124 us
  Pallas kernels  123 us (99%)
    pallas_call x1, Pallas kernels, on_device(): pl.pallas_call(kernel, out_shape=(jax.ShapeDtypeStruct((256, 256), BF16),...  121 us

profile of v3, /device:TPU:1, one launch (start us, length us, event | category | flops | bytes accessed | tf_op | source)
XLA Modules:
  0.0 123.6 jit_solution(3322356563183242306)
XLA Ops:
  0.6 120.8 %lens_step.1 = (bf16[256,256]{1,0:T(8,128)(2,1)}, bf16[256,896]{1,0:T(8,128)(2,1)}, f32[8,128]{1,0:T(8,128)}) custom-call(bf16[8,7168]{1,0:T(8,128)(2,1)} %hid_in.1, bf16[8,7168]{1,0:T(8,128)(2,1)} %fin_in.1, bf16[224,896]{1,0:T(8,128)(2,1)} %tw_in.1, f32[896]{0:T(1024)} %off_in.1, bf16[7168]{0:T(1024)(128)(2,1)} %gain_in.1, bf16[7168,512]{1,0:T(8,128)(2,1)} %unemb.1), custom_call_target="tpu_custom_call" | custom-call | tf_op jit(solution)/shard_map/lens_step/pallas_call | solution.py:562
  121.4 2.2 %finish.1 = (f32[224,896]{1,0:T(8,128)}, f32[896]{0:T(1024)}, f32[8]{0:T(128)}) custom-call(bf16[256,256]{1,0:T(8,128)(2,1)} %get-tuple-element.6.rows, bf16[256,896]{1,0:T(8,128)(2,1)} %get-tuple-element.7.delta, f32[8,128]{1,0:T(8,128)} %get-tuple-element.8.div), custom_call_target="tpu_custom_call" | custom-call | tf_op jit(solution)/shard_map/finish/pallas_call | solution.py:577

commit v4 on v3

--- a/solution.py
+++ b/solution.py
@@ -96,19 +96,25 @@
         copy(land, land, *pair(sem), dev).wait_recv()
 
     def others(n, me):
-        return [(d - 1, lax.rem(me + d, n), lax.rem(me + (n - d), n)) for d in range(1, n)]
+        far_first = sorted(range(1, n), key=lambda d: -min(d, n - d))
+        return [(d - 1, lax.rem(me + d, n), lax.rem(me + (n - d), n)) for d in far_first]
+
+    rings = {id(me): others(n, me) for n, me in ((NZ, z), (NX, x), (NY, y))}
+
+    def others(n, me):
+        return rings[id(me)]
 
     barrier = pltpu.get_barrier_semaphore()
     def slot_of(i, j):
         return lax.div(i, 4) * 16 + j * 4 + lax.rem(i, 4)
 
+    steps = [(i, j) for i in range(NZ) for j in range(NX) if i + j]
+    steps.sort(key=lambda s: -(min(s[0], NZ - s[0]) + min(s[1], NX - s[1])))
     plane = []
-    for i in range(NZ):
-        for j in range(NX):
-            if i + j:
-                ahead = (lax.rem(z + i, NZ), lax.rem(x + j, NX))
-                behind = (lax.rem(z + (NZ - i), NZ), lax.rem(x + (NX - j), NX))
-                plane.append((len(plane), ahead, behind))
+    for i, j in steps:
+        ahead = (lax.rem(z + i, NZ), lax.rem(x + j, NX))
+        behind = (lax.rem(z + (NZ - i), NZ), lax.rem(x + (NX - j), NX))
+        plane.append((len(plane), ahead, behind))
     partners = [(zz * NX + xx, c) for _, (zz, xx), _ in plane]
     group = [(d - 1, (r, lax.rem(c + d, 8)), (r, lax.rem(c + (8 - d), 8))) for d in range(1, 8)]
     partners += [t for _, t, _ in group]
@@ -146,52 +152,57 @@
         send(f_pack, f_z.at[z], (fz_s, fz_r, (j,)), at_z(t))
     f_z[z] = f_pack[...]
 
-    f_first, l_first = ("x", "y"), ("x", "y")
-
-    def own_pieces(buf, flat, s1, r1, s2, r2, sc, rc, firsts):
+    def own_pieces(buf, flat, s1, r1, s2, r2):
         for h in range(2):
             buf[k, y, h, x] = flat[h * 32 : (h + 1) * 32]
         for stage in range(2):
-            for h, first in enumerate(firsts):
+            for h in range(2):
                 piece = buf.at[k, y, h, x]
-                along_x = (first == "x") == (stage == 0)
+                along_x = h == stage
                 n, me, at = (NX, x, at_x) if along_x else (NY, y, at_y)
                 for j, t, _ in others(n, me):
                     sem = (s1, r1, (h, j)) if stage == 0 else (s2, r2, (h, 0, j))
                     send(piece, piece, sem, at(t))
-        for h in range(2):
-            piece = buf.at[k, y, h, x]
-            send(piece, piece, (sc, rc, (h, 0, 0)), sibling)
-
-    def forward(buf, s1, r1, s2, r2, sc, rc, firsts):
+    def to_sibling(buf, yy, h, sc, rc, q):
+        block = buf.at[k, yy, h]
+        send(block, block, (sc, rc, (h, q)), sibling)
+
+    def forward(buf, s1, r1, s2, r2, sc, rc):
         for q in (1, 3, 2):
-            for h, first in enumerate(firsts):
-                if first == "x":
+            for h in range(2):
+                if h == 0:
                     s = lax.rem(x + (NX - q), NX)
                     piece, dev, n2, m2, at2 = buf.at[k, y, h, s], at_x(s), NY, y, at_y
-                    slot = (h, 0, q)
                 else:
                     s = lax.rem(y + (NY - q), NY)
                     piece, dev, n2, m2, at2 = buf.at[k, s, h, x], at_y(s), NX, x, at_x
-                    slot = (h, q, 0)
                 recv(piece, (s1, r1, (h, q - 1)), dev)
                 for j, t, _ in others(n2, m2):
                     send(piece, piece, (s2, r2, (h, q, j)), at2(t))
-                send(piece, piece, (sc, rc, slot), sibling)
-
-    def rest(buf, s2, r2, sc, rc, firsts):
-        for j in (0, 1, 3, 2):
+        to_sibling(buf, y, 0, sc, rc, 0)
+
+    def rest(buf, s2, r2, sc, rc):
+        def half0(q):
+            yy = lax.rem(y + (NY - q), NY)
+            for j in range(NX):
+                xx = lax.rem(x + (NX - j), NX)
+                recv(buf.at[k, yy, 0, xx], (s2, r2, (0, j, q - 1)), at_y(yy))
+            to_sibling(buf, yy, 0, sc, rc, q)
+
+        def half1(j):
+            yy = lax.rem(y + (NY - j), NY)
             for q in (1, 3, 2):
-                for h, first in enumerate(firsts):
-                    if first == "x":
-                        yy, xx = lax.rem(y + (NY - q), NY), lax.rem(x + (NX - j), NX)
-                        dev, slot = at_y(yy), (h, q, j)
-                    else:
-                        yy, xx = lax.rem(y + (NY - j), NY), lax.rem(x + (NX - q), NX)
-                        dev, slot = at_x(xx), (h, j, q)
-                    piece = buf.at[k, yy, h, xx]
-                    recv(piece, (s2, r2, (h, j, q - 1)), dev)
-                    send(piece, piece, (sc, rc, slot), sibling)
+                xx = lax.rem(x + (NX - q), NX)
+                recv(buf.at[k, yy, 1, xx], (s2, r2, (1, j, q - 1)), at_x(xx))
+            to_sibling(buf, yy, 1, sc, rc, j)
+
+        half1(0)
+        half0(1)
+        half1(1)
+        half0(3)
+        half1(3)
+        half0(2)
+        half1(2)
 
     def all_logits(buf, log, sc, rc):
         def step(n, _):
@@ -201,9 +212,7 @@
             @pl.when(n >= NY)
             def _():
                 for h in range(2):
-                    for j in range(4):
-                        xx = lax.rem(x + (NX - j), NX)
-                        recv(buf.at[1 - k, yy, h, xx], (sc, rc, (h, q, j)), sibling)
+                    recv(buf.at[1 - k, yy, h], (sc, rc, (h, q)), sibling)
 
             cc = yy * 2 + kk
             block = pl.ds(pl.multiple_of(cc * COLS, 128), COLS)
@@ -245,7 +254,7 @@
 
     for j, _, s in others(NZ, z):
         recv(f_z.at[s], (fz_s, fz_r, (j,)), at_z(s))
-    own_pieces(f_buf, unpack(f_z[...]), f1_s, f1_r, f2_s, f2_r, fc_s, fc_r, f_first)
+    own_pieces(f_buf, unpack(f_z[...]), f1_s, f1_r, f2_s, f2_r)
     rows_out[...] = rows.T.astype(BF16)
     for p, (h, part) in enumerate(quarters):
         for j, _, s in others(NX, x):
@@ -257,7 +266,7 @@
         z_send(sx, dz, d_s, d_r, 2 * p)
         z_send(sx, dz, d_s, d_r, 2 * p + 1)
     load_off.wait()
-    forward(f_buf, f1_s, f1_r, f2_s, f2_r, fc_s, fc_r, f_first)
+    forward(f_buf, f1_s, f1_r, f2_s, f2_r, fc_s, fc_r)
     base = hid[:, feat].astype(F32) + off[...].reshape(1, COLS) + sx[z]
     gain_part = gains[c]
     for j, _, s in others(NZ, z):
@@ -274,12 +283,12 @@
     f_log[...] = jnp.zeros_like(f_log)
     for j, _, s in others(NZ, z):
         recv(l_z.at[s], (lz_s, lz_r, (j,)), at_z(s))
-    own_pieces(l_buf, unpack(l_z[...]), l1_s, l1_r, l2_s, l2_r, lc_s, lc_r, l_first)
-    forward(l_buf, l1_s, l1_r, l2_s, l2_r, lc_s, lc_r, l_first)
-    rest(f_buf, f2_s, f2_r, fc_s, fc_r, f_first)
+    own_pieces(l_buf, unpack(l_z[...]), l1_s, l1_r, l2_s, l2_r)
+    forward(l_buf, l1_s, l1_r, l2_s, l2_r, lc_s, lc_r)
+    rest(f_buf, f2_s, f2_r, fc_s, fc_r)
     load_u.wait()
     all_logits(f_buf, f_log, fc_s, fc_r)
-    rest(l_buf, l2_s, l2_r, lc_s, lc_r, l_first)
+    rest(l_buf, l2_s, l2_r, lc_s, lc_r)
     all_logits(l_buf, l_log, lc_s, lc_r)
 
     place = lax.broadcasted_iota(jnp.int32, (32, 128), 1)
@@ -489,17 +498,27 @@
     own = sd_z.at[mine8]
     for j, t, _ in others(NZ, z):
         send(own, own, (oz_s, oz_r, (j,)), at_z(t))
-    for j, t, _ in others(NX, x):
-        send(own, own, (ox_s, ox_r, (0, j)), at_x(t))
-    for q, _, s in others(NZ, z):
-        piece = sd_z.at[slot_of(s, x)]
-        recv(piece, (oz_s, oz_r, (q,)), at_z(s))
+
+    def four(hh, xx):
+        return sd_z.at[pl.ds(hh * 16 + xx * 4, 4)]
+
+    for near in range(2):
+        hh = half if near == 0 else 1 - half
+        for i in range(4):
+            s = hh * 4 + i
+
+            @pl.when(s != z)
+            def _():
+                place = lax.rem(z - s + NZ, NZ) - 1
+                piece = sd_z.at[slot_of(s, x)]
+                copy(piece, piece, oz_s.at[place], oz_r.at[place], at_z(s)).wait_recv()
+
         for j, t, _ in others(NX, x):
-            send(piece, piece, (ox_s, ox_r, (q + 1, j)), at_x(t))
-    for q in range(NZ):
+            send(four(hh, x), four(hh, x), (ox_s, ox_r, (near, j)), at_x(t))
+    for near in range(2):
+        hh = half if near == 0 else 1 - half
         for j, _, s in others(NX, x):
-            piece = sd_z.at[slot_of(lax.rem(z + (NZ - q), NZ), s)]
-            recv(piece, (ox_s, ox_r, (q, j)), at_x(s))
+            recv(four(hh, s), (ox_s, ox_r, (near, j)), at_x(s))
     found = sd_z[...].astype(F32)
     sd_out[...] = jnp.concatenate([found[:, :8], found[:, 8:, :384]], axis=2).reshape(256, COLS).astype(BF16)
 
@@ -548,12 +567,12 @@
     ]
     pairs = [
         (31,), (4, 3), (7,),
-        (7,), (2, 3), (2, 4, 3), (2, 4, 4),
-        (7,), (2, 3), (2, 4, 3), (2, 4, 4),
+        (7,), (2, 3), (2, 4, 3), (2, 4),
+        (7,), (2, 3), (2, 4, 3), (2, 4),
         (7,), (3,), (7,),
         (), (3,), (3,), (7,),
         (4,), (2,), (2, 2), (4,), (4,), (4,), (2, 3, 4), (7,),
-        (7,), (8, 3),
+        (7,), (2, 3),
     ]
     sems = [dma((6,))]
     for shape in pairs:

time: 124 us -> 123 us (level); the launches traced: 124 us -> 121 us
  Pallas kernels: 123 us -> 120 us
    pallas_call x1, Pallas kernels: 121 us -> 118 us  [on_device(): pl.pallas_call(kernel, out_shape=(jax.ShapeDtypeStruct((256, 256), BF16),...]
where the time goes in v4:
time: 123 us; the launch traced here: 121 us
  Pallas kernels  120 us (98%)
    pallas_call x1, Pallas kernels, on_device(): pl.pallas_call(kernel, out_shape=(jax.ShapeDtypeStruct((256, 256), BF16),...  118 us

profile of v4, /device:TPU:1, one launch (start us, length us, event | category | flops | bytes accessed | tf_op | source)
XLA Modules:
  0.0 121.0 jit_solution(18092764625864038668)
XLA Ops:
  0.6 118.1 %lens_step.1 = (bf16[256,256]{1,0:T(8,128)(2,1)}, bf16[256,896]{1,0:T(8,128)(2,1)}, f32[8,128]{1,0:T(8,128)}) custom-call(bf16[8,7168]{1,0:T(8,128)(2,1)} %hid_in.1, bf16[8,7168]{1,0:T(8,128)(2,1)} %fin_in.1, bf16[224,896]{1,0:T(8,128)(2,1)} %tw_in.1, f32[896]{0:T(1024)} %off_in.1, bf16[7168]{0:T(1024)(128)(2,1)} %gain_in.1, bf16[7168,512]{1,0:T(8,128)(2,1)} %unemb.1), custom_call_target="tpu_custom_call" | custom-call | tf_op jit(solution)/shard_map/lens_step/pallas_call | solution.py:581
  118.7 2.2 %finish.1 = (f32[224,896]{1,0:T(8,128)}, f32[896]{0:T(1024)}, f32[8]{0:T(128)}) custom-call(bf16[256,256]{1,0:T(8,128)(2,1)} %get-tuple-element.6.rows, bf16[256,896]{1,0:T(8,128)(2,1)} %get-tuple-element.7.delta, f32[8,128]{1,0:T(8,128)} %get-tuple-element.8.div), custom_call_target="tpu_custom_call" | custom-call | tf_op jit(solution)/shard_map/finish/pallas_call | solution.py:596

commit v5 on v4

--- a/solution.py
+++ b/solution.py
@@ -116,7 +116,7 @@
         behind = (lax.rem(z + (NZ - i), NZ), lax.rem(x + (NX - j), NX))
         plane.append((len(plane), ahead, behind))
     partners = [(zz * NX + xx, c) for _, (zz, xx), _ in plane]
-    group = [(d - 1, (r, lax.rem(c + d, 8)), (r, lax.rem(c + (8 - d), 8))) for d in range(1, 8)]
+    group = [(d - 1, (r, lax.rem(c + d, 8)), (r, lax.rem(c + (8 - d), 8))) for d in (4, 3, 5, 2, 6, 1, 7)]
     partners += [t for _, t, _ in group]
     for p in partners:
         pl.semaphore_signal(barrier, inc=1, device_id=p, device_id_type=MESH)
@@ -461,12 +461,12 @@
         return 0
 
     lax.fori_loop(0, NX, add0, 0)
+    sl_x[NX - 1] = slope_sum(*over_y)
+    slope_send(*over_x)
     eights = [pl.ds(8 * q, 8) for q in range(4)]
     for q, part in enumerate(eights):
         for j, t, _ in others(NX, x):
             send(r0.at[t, part], rx0.at[j, part], (g2_s, g2_r, (0, j, q)), at_x(t))
-    sl_x[NX - 1] = slope_sum(*over_y)
-    slope_send(*over_x)
 
     for i in range(NY):
         x_near(i).wait_recv()
@@ -475,6 +475,8 @@
     for q, part in enumerate(eights):
         for i in range(NY - 1):
             send(r1.at[i, part], ry1.at[i, part], (g2_s, g2_r, (1, i, q)), at_y(block_y(i)))
+    sl_z[NZ - 1] = slope_sum(*over_x)
+    slope_send(*over_z)
     for q, part in enumerate(eights):
         for j, _, s in others(NX, x):
             recv(rx0.at[j, part], (g2_s, g2_r, (0, j, q)), at_x(s))
@@ -484,13 +486,11 @@
             recv(ry1.at[i, part], (g2_s, g2_r, (1, i, q)), at_y(block_y(i)))
         sz[4 + q] = r1[NY - 1, part] + ry1[0, part] + ry1[1, part] + ry1[2, part]
         z_send(sz, rz, gz_s, gz_r, 4 + q)
-    sl_z[NZ - 1] = slope_sum(*over_x)
-    slope_send(*over_z)
+    cols[...] = jnp.concatenate([slope_sum(*over_z), jnp.zeros((120, 256), F32)], axis=0).T
     state_grad = sz[z]
     for j, _, s in others(NZ, z):
         recv(rz.at[j], (gz_s, gz_r, (j,)), at_z(s))
         state_grad = state_grad + rz[j]
-    cols[...] = jnp.concatenate([slope_sum(*over_z), jnp.zeros((120, 256), F32)], axis=0).T
     inverse = inv_cols[mine, 0:1]
     slope = cols[mine, 0:1] / D
     delta = inverse * (gain_part * state_grad) - l_state[...] * (inverse * inverse * slope)

time: 123 us -> 121 us (0.984); the launches traced: 121 us -> 121 us
  no operation moved by 1% of the time
where the time goes in v5:
time: 121 us
  Pallas kernels  121 us (100%)
    pallas_call x1, Pallas kernels, on_device(): pl.pallas_call(kernel, out_shape=(jax.ShapeDtypeStruct((256, 256), BF16),...  119 us

profile of v5, /device:TPU:1, one launch (start us, length us, event | category | flops | bytes accessed | tf_op | source)
XLA Modules:
  0.0 121.4 jit_solution(10366830224063991744)
XLA Ops:
  0.6 118.5 %lens_step.1 = (bf16[256,256]{1,0:T(8,128)(2,1)}, bf16[256,896]{1,0:T(8,128)(2,1)}, f32[8,128]{1,0:T(8,128)}) custom-call(bf16[8,7168]{1,0:T(8,128)(2,1)} %hid_in.1, bf16[8,7168]{1,0:T(8,128)(2,1)} %fin_in.1, bf16[224,896]{1,0:T(8,128)(2,1)} %tw_in.1, f32[896]{0:T(1024)} %off_in.1, bf16[7168]{0:T(1024)(128)(2,1)} %gain_in.1, bf16[7168,512]{1,0:T(8,128)(2,1)} %unemb.1), custom_call_target="tpu_custom_call" | custom-call | tf_op jit(solution)/shard_map/lens_step/pallas_call | solution.py:581
  119.1 2.2 %finish.1 = (f32[224,896]{1,0:T(8,128)}, f32[896]{0:T(1024)}, f32[8]{0:T(128)}) custom-call(bf16[256,256]{1,0:T(8,128)(2,1)} %get-tuple-element.6.rows, bf16[256,896]{1,0:T(8,128)(2,1)} %get-tuple-element.7.delta, f32[8,128]{1,0:T(8,128)} %get-tuple-element.8.div), custom_call_target="tpu_custom_call" | custom-call | tf_op jit(solution)/shard_map/finish/pallas_call | solution.py:596
